TPU v7x, 256 devices: a whole 4x4x8 slice. The times are simulated.
256 devices in a mesh: section: 2 (over core), fsdp: 2 (over z_lo), tok: 64 (over x, z_hi, y).
Axes of the slice: x: 4, y: 4, z: 8 (z_hi: 4, z_lo: 2; z = z_hi * 2 + z_lo), core: 2. Of those that a mesh axis runs over, the one named last changes fastest.
Arguments:
- hidden: bfloat16 [4, 256, 3072], P(None, 'tok'), may hold values from -6 to 6
- lengths: int32 [4], replicated, may hold values from 1 to 256, 768 in all
- text_count: int32 [1], replicated, may hold values from 1 to 256
- timestep: int32 [1], replicated, may hold values from 0 to 49
- mod_table: bfloat16 [2, 50, 6, 3072], P('section'), may hold values from -3 to 3
- w_qkv: bfloat16 [2, 3072, 3, 1536], P('section', 'tok', None, 'fsdp'), may hold values from -0.109375 to 0.109375
- w_out: bfloat16 [2, 3072, 1536], P('section', 'tok', 'fsdp'), may hold values from -0.15625 to 0.15625
- qk_gain: float32 [2, 2, 64], P('section'), may hold values from 0.5 to 2
- stale_cache: bfloat16 [2, 2, 4, 256, 1536], P('section', None, None, None, 'fsdp'), may hold values from -6 to 6
Outputs:
- layer_out: bfloat16 [2, 4, 256, 3072], P('section', None, 'tok')
- new_cache: bfloat16 [2, 2, 4, 256, 1536], P('section', None, None, None, 'fsdp')
Inputs may be any that keep to these rules, and one draw needn't show every extreme that they name: The lengths sum to 768; one patch is full with exactly 256 live tokens.
All inputs are finite; a program needn't handle non-finite values.
Results may differ from a plain program's by a relative error of at most 0.012.
Values may be sent and summed in bfloat16 or wider, within the bound.
A program may use at most 128 MiB of HBM per device.

v0:
```python
import jax
import jax.numpy as jnp
from jax import lax
from jax.sharding import PartitionSpec as P

HEAD_DIM = 64


def from_behind(block, axis, distance):
    devices = range(lax.axis_size(axis))
    route = [(i - distance, i) for i in devices if i - distance in devices]
    return lax.ppermute(block, axis, route)


def layer_norm(values, eps):
    mean = jnp.mean(values, axis=-1, keepdims=True)
    centred = values - mean
    spread = jnp.mean(centred * centred, axis=-1, keepdims=True)
    return centred * lax.rsqrt(spread + eps)


def modulate(inputs, positions, modulation, text_total):
    is_text = (positions < text_total)[:, None]
    shift = jnp.where(is_text, modulation[3], modulation[0])
    scale = jnp.where(is_text, modulation[4], modulation[1])
    gate = jnp.where(is_text, modulation[5], modulation[2])
    normed = layer_norm(inputs, 1e-05)
    return ((normed * (1.0 + scale) + shift).astype(jnp.bfloat16), gate)


def project_heads(mixed, gains):
    queries = (layer_norm(mixed[:, 0], 1e-06) * gains[0]).astype(jnp.bfloat16)
    keys_new = (layer_norm(mixed[:, 1], 1e-06) * gains[1]).astype(jnp.bfloat16)
    values_new = mixed[:, 2].astype(jnp.bfloat16)
    return (queries, keys_new, values_new)


def attend(queries, keys_all, values_all, key_live):
    scores = jnp.einsum(
        "qhd,khd->hqk", queries, keys_all, preferred_element_type=jnp.float32
    ) * HEAD_DIM ** (-0.5)
    scores = jnp.where(key_live[None, None, :], scores, -jnp.inf)
    top = jnp.max(scores, axis=-1, keepdims=True)
    expo = jnp.exp(scores - top)
    weights = (expo / jnp.sum(expo, axis=-1, keepdims=True)).astype(jnp.bfloat16)
    return jnp.einsum(
        "hqk,khd->qhd", weights, values_all, preferred_element_type=jnp.float32
    ).astype(jnp.bfloat16)


def local(hidden, lengths, text_count, timestep, mod_table, w_qkv, w_out, qk_gain, stale_cache):
    section_index = lax.axis_index("section")
    section_count = lax.axis_size("section")
    tok_index = lax.axis_index("tok")
    tok_count = lax.axis_size("tok")
    patches, cap_dev, width = hidden.shape
    cap_all = cap_dev * tok_count
    local_width = w_qkv.shape[3]
    heads_local = local_width // HEAD_DIM
    rows_local = jnp.arange(cap_dev, dtype=jnp.int32) + tok_index * cap_dev
    key_rows = jnp.arange(cap_all, dtype=jnp.int32)
    key_live = (key_rows[None, :] < lengths[:, None]).reshape(-1)
    offsets = jnp.cumsum(lengths) - lengths
    modulation = lax.dynamic_index_in_dim(mod_table[0], timestep[0], 0, keepdims=False).astype(
        jnp.float32
    )
    gains = qk_gain[0]
    shard_in = w_qkv[0].reshape(w_qkv.shape[1], 3 * local_width)
    out_local = w_out[0]
    weight_in, weight_out = (
        lax.all_gather(shard_in, "tok", axis=0, tiled=True),
        lax.all_gather(out_local, "tok", axis=0, tiled=True),
    )
    cache_keys = stale_cache[0, 0]
    cache_values = stale_cache[0, 1]
    out_states = jnp.zeros((patches, cap_dev, width), jnp.bfloat16)
    incoming = jnp.zeros((cap_dev, width), jnp.bfloat16)
    ticks = patches + section_count - 1
    for tick in range(ticks):
        patch = tick - section_index
        is_live = (patch >= 0) & (patch < patches)
        patch_slot = jnp.clip(patch, 0, patches - 1)
        own_states = hidden[min(tick, patches - 1)]
        inputs = jnp.where(section_index == 0, own_states, incoming).astype(jnp.float32)
        row_live = rows_local < lengths[patch_slot]
        modded, gate = modulate(inputs, offsets[patch_slot] + rows_local, modulation, text_count[0])
        mixed = jnp.dot(modded, weight_in, preferred_element_type=jnp.float32)
        mixed = mixed.reshape(cap_dev, 3, heads_local, HEAD_DIM)
        queries, keys_new, values_new = project_heads(mixed, gains)
        keys_new = jnp.where(row_live[:, None, None], keys_new, jnp.zeros_like(keys_new)).reshape(
            cap_dev, local_width
        )
        values_new = jnp.where(
            row_live[:, None, None], values_new, jnp.zeros_like(values_new)
        ).reshape(cap_dev, local_width)
        fresh_keys, fresh_values = (
            lax.all_gather(keys_new, "tok", axis=0, tiled=True),
            lax.all_gather(values_new, "tok", axis=0, tiled=True),
        )
        cache_keys = jnp.where(
            is_live,
            lax.dynamic_update_index_in_dim(cache_keys, fresh_keys, patch_slot, 0),
            cache_keys,
        )
        cache_values = jnp.where(
            is_live,
            lax.dynamic_update_index_in_dim(cache_values, fresh_values, patch_slot, 0),
            cache_values,
        )
        attended = attend(
            queries,
            cache_keys.reshape(-1, heads_local, HEAD_DIM),
            cache_values.reshape(-1, heads_local, HEAD_DIM),
            key_live,
        ).reshape(cap_dev, local_width)
        partial_out = lax.dot_general(
            attended, weight_out, (((1,), (1,)), ((), ())), preferred_element_type=jnp.float32
        )
        projected = lax.psum(partial_out.astype(jnp.bfloat16), "fsdp").astype(jnp.float32)
        result = jnp.where(row_live[:, None], inputs + gate * projected, 0.0).astype(jnp.bfloat16)
        out_states = jnp.where(
            is_live, lax.dynamic_update_index_in_dim(out_states, result, patch_slot, 0), out_states
        )
        if tick + 1 < ticks:
            incoming = from_behind(result, "section", 1)
    return (out_states[None], jnp.stack([cache_keys, cache_values])[None])


def solution(mesh):
    in_specs = (
        P(None, "tok", None),
        P(),
        P(),
        P(),
        P("section", None, None, None),
        P("section", "tok", None, "fsdp"),
        P("section", "tok", "fsdp"),
        P("section", None, None),
        P("section", None, None, None, "fsdp"),
    )
    out_specs = (P("section", None, "tok", None), P("section", None, None, None, "fsdp"))
    return jax.shard_map(local, mesh=mesh, in_specs=in_specs, out_specs=out_specs, check_vma=False)
```

profile of v0, /device:TPU:40, one launch (start us, length us, event | category | flops | bytes accessed | tf_op | source)
XLA Modules:
  0.0 2399.3 jit_solution(7647845240221618332)
XLA Ops:
  25.0 4.4 fusion.206
  29.4 135.6 %all-gather.14.cloned.1.call-done = bf16[3072,2304]{1,0:T(8,128)(2,1)} async-done(((bf16[48,2304]{1,0:T(8,128)(2,1)}), bf16[3072,2304]{1,0:T(8,128)(2,1)}) %all-gather.14.cloned.1.call-update) | async-done | bytes 14155792 | tf_op jit(solution)/shard_map/all_gather | solution.py:71
  165.1 18.7 copy.136
  183.8 9.0 fusion.116
  194.0 198.5 %all-gather.1 = bf16[64,4,768]{2,1,0:T(4,128)(2,1)} all-gather(bf16[1,4,768]{2,1,0:T(4,128)(2,1)S(1)} %get-tuple-element.70), channel_id=1, replica_groups=mesh['section'=2,'fsdp'=2,'tok'=64] {'tok'}, dimensions={0}, use_global_device_ids=true | all-gather | bytes 399360 | tf_op jit(solution)/shard_map/all_gather | solution.py:98
  394.3 201.3 %all-gather.2 = bf16[64,4,768]{2,1,0:T(4,128)(2,1)} all-gather(bf16[1,4,768]{2,1,0:T(4,128)(2,1)S(1)} %get-tuple-element.69), channel_id=1, replica_groups=mesh['section'=2,'fsdp'=2,'tok'=64] {'tok'}, dimensions={0}, use_global_device_ids=true | all-gather | bytes 399360 | tf_op jit(solution)/shard_map/all_gather | solution.py:97
  619.6 9.4 psum.35
  631.7 7.6 fusion.105
  649.1 195.5 %all-gather.4 = bf16[64,4,768]{2,1,0:T(4,128)(2,1)} all-gather(bf16[1,4,768]{2,1,0:T(4,128)(2,1)S(1)} %get-tuple-element.67), channel_id=1, replica_groups=mesh['section'=2,'fsdp'=2,'tok'=64] {'tok'}, dimensions={0}, use_global_device_ids=true | all-gather | bytes 399360 | tf_op jit(solution)/shard_map/all_gather | solution.py:97
  856.3 197.8 %all-gather.3 = bf16[64,4,768]{2,1,0:T(4,128)(2,1)} all-gather(bf16[1,4,768]{2,1,0:T(4,128)(2,1)S(1)} %get-tuple-element.68), channel_id=1, replica_groups=mesh['section'=2,'fsdp'=2,'tok'=64] {'tok'}, dimensions={0}, use_global_device_ids=true | all-gather | bytes 399360 | tf_op jit(solution)/shard_map/all_gather | solution.py:98
  1068.9 6.9 psum.36
  1078.4 7.6 fusion.107
  1095.8 195.7 %all-gather.6 = bf16[64,4,768]{2,1,0:T(4,128)(2,1)} all-gather(bf16[1,4,768]{2,1,0:T(4,128)(2,1)S(1)} %get-tuple-element.65), channel_id=1, replica_groups=mesh['section'=2,'fsdp'=2,'tok'=64] {'tok'}, dimensions={0}, use_global_device_ids=true | all-gather | bytes 399360 | tf_op jit(solution)/shard_map/all_gather | solution.py:97
  1296.7 3.8 reshape.589
  1303.3 197.4 %all-gather.5 = bf16[64,4,768]{2,1,0:T(4,128)(2,1)} all-gather(bf16[1,4,768]{2,1,0:T(4,128)(2,1)S(1)} %get-tuple-element.66), channel_id=1, replica_groups=mesh['section'=2,'fsdp'=2,'tok'=64] {'tok'}, dimensions={0}, use_global_device_ids=true | all-gather | bytes 399360 | tf_op jit(solution)/shard_map/all_gather | solution.py:98
  1515.5 8.7 psum.37
  1526.9 7.6 fusion.109
  1544.3 195.8 %all-gather.8 = bf16[64,4,768]{2,1,0:T(4,128)(2,1)} all-gather(bf16[1,4,768]{2,1,0:T(4,128)(2,1)S(1)} %get-tuple-element.63), channel_id=1, replica_groups=mesh['section'=2,'fsdp'=2,'tok'=64] {'tok'}, dimensions={0}, use_global_device_ids=true | all-gather | bytes 399360 | tf_op jit(solution)/shard_map/all_gather | solution.py:97
  1751.8 197.5 %all-gather.7 = bf16[64,4,768]{2,1,0:T(4,128)(2,1)} all-gather(bf16[1,4,768]{2,1,0:T(4,128)(2,1)S(1)} %get-tuple-element.64), channel_id=1, replica_groups=mesh['section'=2,'fsdp'=2,'tok'=64] {'tok'}, dimensions={0}, use_global_device_ids=true | all-gather | bytes 399360 | tf_op jit(solution)/shard_map/all_gather | solution.py:98
  1964.2 6.9 psum.38
  1974.5 7.0 fusion.111
  1984.1 185.9 %all-gather.10 = bf16[64,4,768]{2,1,0:T(4,128)(2,1)S(1)} all-gather(bf16[1,4,768]{2,1,0:T(4,128)(2,1)S(1)} %get-tuple-element.51), channel_id=1, replica_groups=mesh['section'=2,'fsdp'=2,'tok'=64] {'tok'}, dimensions={0}, use_global_device_ids=true | all-gather | bytes 399360 | tf_op jit(solution)/shard_map/all_gather | solution.py:97
  2170.8 187.8 %all-gather.9 = bf16[64,4,768]{2,1,0:T(4,128)(2,1)S(1)} all-gather(bf16[1,4,768]{2,1,0:T(4,128)(2,1)} %get-tuple-element.52), channel_id=1, replica_groups=mesh['section'=2,'fsdp'=2,'tok'=64] {'tok'}, dimensions={0}, use_global_device_ids=true | all-gather | bytes 399360 | tf_op jit(solution)/shard_map/all_gather | solution.py:98
  2380.2 8.8 psum.39
  (297 shorter events, 187.9 us)
Async XLA Ops:
  7.2 157.9 %all-gather.14.cloned.1.call-start = ((), (), s32[]{:S(2)}) async-start(), calls=%async_computation | async-start | bytes 14376960 | tf_op jit(solution)/shard_map/all_gather | solution.py:71
  9.0 606.9 %all-gather.16.cloned.1.call-start = ((), (), s32[]{:S(2)}) async-start(), calls=%async_computation.1 | async-start | bytes 4792320 | tf_op jit(solution)/shard_map/all_gather | solution.py:72
  12.7 598.3 %copy-start.20 = (f32[64]{0:T(128)}, f32[64]{0:T(128)S(1)}, u32[]{:S(2)}) copy-start(f32[64]{0:T(128)S(1)} %get-tuple-element.49) | copy-start | bytes 772
  29.4 1941.7 %copy-start.3 = (f32[1,1,1,3072]{3,1,2,0:T(1,128)}, f32[1,1,1,3072]{3,1,2,0:T(1,128)S(1)}, u32[]{:S(2)}) copy-start(f32[1,1,1,3072]{3,1,2,0:T(1,128)S(1)} %get-tuple-element.47) | copy-start | bytes 36868
  165.1 18.7 copy-start.5
  629.2 2.1 collective-permute-start
  631.2 8.2 copy-start.28
  849.8 3.8 copy-start.21
  1065.3 10.6 copy-start.29
  1065.3 10.6 copy-start.38
  1075.9 2.1 collective-permute-start.1
  1077.8 8.2 copy-start.30
  1296.7 3.8 copy-start.22
  1511.9 12.4 copy-start.31
  1511.9 12.4 copy-start.37
  1524.4 2.1 collective-permute-start.2
  1526.3 8.2 copy-start.32
  1745.3 3.8 copy-start.23
  1960.5 10.6 copy-start.33
  1960.5 10.6 copy-start.36
  1971.2 10.3 copy-start
  1971.2 2.5 collective-permute-start.3
  1973.1 8.4 copy-start.26
  1974.5 8.9 copy-start.34
  (21 other events, 41.0 us)
Sparse Core Ops, SparseCore 0:
  11.2 153.8 all-gather.13
  168.3 87.9 all-gather.15
where the time goes:
time: 2400 us
  blocking collectives  1990 us (83%)
  waiting for transfers between devices  137 us (6%)
  local copies, waits for them, and re-layouts  126 us (5%)
  matrix products  76.5 us (3%)
  other arithmetic  44.9 us (2%)
    all_gather x5, blocking collectives, local(): lax.all_gather(values_new, 'tok', axis=0, tiled=True)  979 us
    all_gather x5, blocking collectives, local(): lax.all_gather(keys_new, 'tok', axis=0, tiled=True)  974 us
    all_gather x1, waiting for transfers between devices, local(): lax.all_gather(shard_in, 'tok', axis=0, tiled=True)  136 us
  transfers between devices with their start and end apart: 6, of which 4 were waited for; matrix products, arithmetic and copies ran while one was open for 3% of the time, Pallas kernels for 0%

commit v1 on v0

v1 whole, which is shorter than its diff:
```python
import functools

import jax
import jax.numpy as jnp
from jax import lax
from jax.experimental import pallas as pl
from jax.experimental.pallas import tpu as pltpu
from jax.sharding import PartitionSpec as P

HEAD_DIM = 64
F32 = jnp.float32
BF16 = jnp.bfloat16
HIDE = -1e30
COPIES = 10


def bits(number):
    assert number & (number - 1) == 0
    return number.bit_length() - 1


def matmul(a, b):
    return jnp.dot(a, b, preferred_element_type=F32)


def matmul_t(a, b):
    return lax.dot_general(a, b, (((1,), (1,)), ((), ())), preferred_element_type=F32)


def pick(index, values):
    out = jnp.zeros(index.shape, jnp.int32)
    for at, value in enumerate(values):
        out = jnp.where(index == at, value, out)
    return out


def relay(n, nf, patches, cd, hid, lens, text, mod, wq, wo, gain, stale, lo, cache,
          hmine, hbuf, xb, xs, mb, wmine, wbuf, wobuf, kv, zb, cb, ab, xo, ob, fin, stl, old, sends, recvs, send_w, recv_w, gate):
    width = hid.shape[-1]
    rows_w = wq.shape[0]
    local = wq.shape[2]
    hl = local // n
    hc = hl // HEAD_DIM
    groups = n * n
    ranks = nf * n
    out_w = width // ranks
    run = n * cd
    rows = patches * run
    cap = groups * run
    own_rows = patches * cd

    s, f, t = lax.axis_index("section"), lax.axis_index("fsdp"), lax.axis_index("tok")
    x, z, y = t // (n * n), (t // n) % n, t % n
    g = x * n + y
    k = f * n + z

    def to(x_, z_, y_, f_=None, s_=None):
        return {"section": s if s_ is None else s_, "fsdp": f if f_ is None else f_, "tok": (x_ * n + z_) * n + y_}

    def remote(src, dst, which, target):
        return pltpu.make_async_remote_copy(
            src_ref=src, dst_ref=dst, send_sem=sends.at[which], recv_sem=recvs.at[which],
            device_id=target, device_id_type=pl.DeviceIdType.MESH)

    def sent(ref, which):
        pltpu.make_async_copy(ref, ref, sends.at[which]).wait()

    def arrived(ref, which):
        pltpu.make_async_copy(ref, ref, recvs.at[which]).wait()

    HID, WA, WO, KV, Z, C, A, X, FIN, STALE = range(COPIES)

    fetch = pltpu.make_async_copy(stale, stl, recvs.at[STALE])
    fetch.start()

    @pl.when(s == 0)
    def _():
        hmine[...] = hid[...].reshape(own_rows, width)

        def send(z_, c):
            same = (z_ == z) & (z == y)

            @pl.when(same)
            def _():
                pltpu.make_async_copy(hmine, hbuf.at[y], recvs.at[HID]).start()

            @pl.when(jnp.logical_not(same))
            def _():
                remote(hmine, hbuf.at[y], HID, to(x, z_, z)).start()
            return c
        lax.fori_loop(0, n, send, 0)

    for z_ in range(n):
        for at, part in enumerate((2, 1, 0)):
            wmine[z_, :, at * hl:(at + 1) * hl] = wq[:, part, z_ * hl:(z_ + 1) * hl]

    def send(d, c):
        z_ = (z + d) % n
        remote(wmine.at[z_], wbuf.at[x, z, y], WA, to(x, z_, y)).start()
        return c
    lax.fori_loop(1, n, send, 0)
    pltpu.make_async_copy(wmine.at[z], wbuf.at[x, z, y], recvs.at[WA]).start()
    arrived(wmine, WA)

    @pl.when(s == 1)
    def _():
        pl.semaphore_wait(gate, 1)

    def send(d, c):
        g_ = (g + d) % groups
        pltpu.make_async_remote_copy(
            src_ref=wbuf.at[x, :, y], dst_ref=wbuf.at[x, :, y], send_sem=send_w.at[g_ // n], recv_sem=recv_w.at[x],
            device_id=to(g_ // n, z, g_ % n), device_id_type=pl.DeviceIdType.MESH).start()
        return c
    lax.fori_loop(1, groups, send, 0)

    per = (n * n * n) // ranks
    kk, place = t // per, t % per
    f_o, z_o = kk // n, kk % n

    def send(g_, c):
        same = (f_o == f) & (z_o == z) & (g_ == g)

        @pl.when(same)
        def _():
            pltpu.make_async_copy(wo, wobuf.at[f * per + place], recvs.at[WO]).start()

        @pl.when(jnp.logical_not(same))
        def _():
            remote(wo, wobuf.at[f * per + place], WO, to(g_ // n, z_o, g_ % n, f_)).start()
        return c
    f_ = f_o
    lax.fori_loop(0, groups, send, 0)

    length = [lens[p] for p in range(patches)]
    start = [sum(length[:p], jnp.int32(0)) for p in range(patches)]

    def about(first, count):
        row = first + lax.broadcasted_iota(jnp.int32, (count, 1), 0)
        row_patch = row >> bits(run)
        slot = g * run + (row & (run - 1))
        return slot < pick(row_patch, length), (pick(row_patch, start) + slot) < text[0]

    live, is_text = about(0, rows)

    r0 = lax.broadcasted_iota(jnp.int32, (rows, rows), 0)
    r1 = lax.broadcasted_iota(jnp.int32, (rows, rows), 1)

    def flipped(r):
        p_, y_, i_ = r >> bits(run), (r >> bits(cd)) & (n - 1), r & (cd - 1)
        return (y_ * patches + p_) * cd + i_

    @pl.when(s == 0)
    def _():
        arrived(hbuf, HID)
        order = (flipped(r0) == r1).astype(BF16)
        xs[...] = matmul(order, hbuf[...].reshape(rows, width)).astype(BF16)

    @pl.when(s == 1)
    def _():
        arrived(xb, X)
        for k_ in range(ranks):
            xs[:, k_ * out_w:(k_ + 1) * out_w] = xb[k_]

    step = min(16, rows)
    for at in range(0, rows, step):
        here = slice(at, at + step)
        values = xs[here, :].astype(F32)
        mean = jnp.mean(values, axis=1, keepdims=True)
        centred = values - mean
        spread = jnp.mean(centred * centred, axis=1, keepdims=True)
        normed = centred * lax.rsqrt(spread + 1e-05)
        text_here = about(at, step)[1]
        scale = jnp.where(text_here, mod[4:5, :], mod[1:2, :])
        shift = jnp.where(text_here, mod[3:4, :], mod[0:1, :])
        mb[here, :] = (normed * (1.0 + scale) + shift).astype(BF16)

    chunk = groups * rows_w
    total = None
    for d in range(n):
        x_ = (x + d) % n
        if d == 0:
            ref = wbuf.at[x_, :, pl.ds(0, n - 1)]
        else:
            ref = wbuf.at[x_]
        pltpu.make_async_copy(ref, ref, recv_w.at[x_]).wait()
        columns = pl.ds(pl.multiple_of(x_ * chunk, chunk), chunk)
        part = matmul(mb[:, columns], wbuf[x_].reshape(chunk, 3 * hl))
        total = part if total is None else total + part

    @pl.when(s == 0)
    def _():
        pl.semaphore_signal(gate, 1, device_id=to(x, z, y, f, 1), device_id_type=pl.DeviceIdType.MESH)

    head = lax.broadcasted_iota(jnp.int32, (1, hl), 1) >> bits(HEAD_DIM)

    def head_norm(values, gains):
        mean = jnp.zeros_like(values)
        for h in range(hc):
            here = head == h
            mean = jnp.where(here, jnp.sum(jnp.where(here, values, 0.0), axis=1, keepdims=True) / HEAD_DIM, mean)
        centred = values - mean
        square = centred * centred
        spread = jnp.zeros_like(values)
        for h in range(hc):
            here = head == h
            spread = jnp.where(here, jnp.sum(jnp.where(here, square, 0.0), axis=1, keepdims=True) / HEAD_DIM, spread)
        return centred * lax.rsqrt(spread + 1e-06) * jnp.concatenate([gains] * hc, axis=1)

    value_new = jnp.where(live, total[:, :hl], 0.0)
    key_new = jnp.where(live, head_norm(total[:, hl:2 * hl], gain[1:2, :]), 0.0)
    query = head_norm(total[:, 2 * hl:], gain[0:1, :])
    kv[g] = jnp.concatenate([value_new, key_new], axis=1).astype(BF16)

    def send(d, c):
        g_ = (g + d) % groups
        remote(kv.at[g], kv.at[g], KV, to(g_ // n, z, g_ % n)).start()
        return c
    lax.fori_loop(1, groups, send, 0)

    def send(d, c):
        z_ = (z + d) % n
        remote(kv.at[g], zb.at[z], Z, to(x, z_, y)).start()
        return c
    lax.fori_loop(1, n, send, 0)
    pltpu.make_async_copy(kv.at[g], zb.at[z], recvs.at[Z]).start()

    query = jnp.concatenate([jnp.zeros((rows, hl), F32), query], axis=1)
    lane = lax.broadcasted_iota(jnp.int32, (1, 2 * hl), 1)
    queries = jnp.concatenate(
        [jnp.where(((lane - hl) >> bits(HEAD_DIM)) == h, query, 0.0) for h in range(hc)], axis=0).astype(BF16)
    query_row = lax.broadcasted_iota(jnp.int32, (hc * rows, 1), 0)
    query_patch = (query_row & (rows - 1)) >> bits(run)
    column = lax.broadcasted_iota(jnp.int32, (1, patches * cap), 1)

    fetch.wait()
    for z_ in range(n):
        @pl.when(z == z_)
        def _(z_=z_):
            mine = slice(z_ * hl, (z_ + 1) * hl)
            both = jnp.concatenate([stl[1, :, :, mine], stl[0, :, :, mine]], axis=2)
            old[...] = both.reshape(patches * cap, 2 * hl)
    old_patch = column >> bits(cap)
    old_seen = ((column & (cap - 1)) < pick(old_patch, length))
    score_old = matmul_t(queries, old[...]) * HEAD_DIM ** (-0.5)
    score_old = jnp.where(old_seen & (old_patch > query_patch), score_old, HIDE)
    top_old = jnp.max(score_old, axis=1, keepdims=True)

    arrived(zb, Z)
    both = jnp.concatenate([zb[z_][:, hl:] for z_ in range(n)], axis=1)
    cb[0] = both.reshape(patches, run, local)
    both = jnp.concatenate([zb[z_][:, :hl] for z_ in range(n)], axis=1)
    cb[1] = both.reshape(patches, run, local)
    spot = pl.ds(pl.multiple_of(g * run, run), run)

    def send(d, c):
        g_ = (g + d) % groups
        remote(cb, cache.at[:, :, spot], C, to(g_ // n, z, g_ % n)).start()
        return c
    lax.fori_loop(1, groups, send, 0)
    pltpu.make_async_copy(cb, cache.at[:, :, spot], recvs.at[C]).start()

    most = kv.at[pl.ds(0, groups - 1)]
    arrived(most, KV)
    new = kv[...].reshape(patches * cap, 2 * hl)
    new_patch = (column >> bits(run)) & (patches - 1)
    new_slot = (column >> bits(rows)) * run + (column & (run - 1))
    new_seen = new_slot < pick(new_patch, length)
    score_new = matmul_t(queries, new) * HEAD_DIM ** (-0.5)
    score_new = jnp.where(new_seen & (new_patch <= query_patch), score_new, HIDE)
    top = jnp.maximum(top_old, jnp.max(score_new, axis=1, keepdims=True))
    expo_old, expo_new = jnp.exp(score_old - top), jnp.exp(score_new - top)
    norm = 1.0 / (jnp.sum(expo_old, axis=1, keepdims=True) + jnp.sum(expo_new, axis=1, keepdims=True))
    taken = matmul((expo_old * norm).astype(BF16), old[...]) + matmul((expo_new * norm).astype(BF16), new)
    attended = jnp.zeros((rows, hl), F32)
    for h in range(hc):
        attended = jnp.where(head == h, taken[h * rows:(h + 1) * rows, :hl], attended)
    ab[k] = attended.astype(BF16)

    def send(d, c):
        k_ = (k + d) % ranks
        remote(ab.at[k], ab.at[k], A, to(x, k_ % n, y, k_ // n)).start()
        return c
    lax.fori_loop(1, ranks, send, 0)

    arrived(wobuf, WO)
    arrived(ab.at[pl.ds(0, ranks - 1)], A)
    projected = None
    for f_ in range(nf):
        left = jnp.concatenate([ab[f_ * n + z_] for z_ in range(n)], axis=1)
        part = matmul_t(left, wobuf[f_ * per:(f_ + 1) * per].reshape(out_w, local))
        projected = part if projected is None else projected + part
    columns = pl.ds(pl.multiple_of(k * out_w, out_w), out_w)
    gated = jnp.where(is_text, mod[5:6, columns], mod[2:3, columns])
    result = jnp.where(live, xs[:, columns].astype(F32) + gated * projected, 0.0).astype(BF16)

    @pl.when(s == 0)
    def _():
        xo[...] = result

        def send(k_, c):
            remote(xo, xb.at[k], X, to(x, k_ % n, y, k_ // n, 1)).start()
            return c
        lax.fori_loop(0, ranks, send, 0)

    back = (r0 == flipped(r1)).astype(BF16)
    ob[...] = matmul(back, result).astype(BF16).reshape(n, own_rows, out_w)

    def send(j, c):
        y_, f_ = j % n, j // n
        same = (y_ == y) & (z == y) & (f_ == f)

        @pl.when(same)
        def _():
            pltpu.make_async_copy(ob.at[y_], fin.at[k], recvs.at[FIN]).start()

        @pl.when(jnp.logical_not(same))
        def _():
            remote(ob.at[y_], fin.at[k], FIN, to(x, y, y_, f_)).start()
        return c
    lax.fori_loop(0, ranks, send, 0)
    arrived(fin, FIN)
    lo[...] = jnp.concatenate([fin[k_] for k_ in range(ranks)], axis=1).reshape(patches, cd, width)
    arrived(cache, C)

    @pl.when(s == 0)
    def _():
        @pl.when(z == y)
        def _():
            sent(hbuf.at[pl.ds(0, n - 1)], HID)

        @pl.when(z != y)
        def _():
            sent(hbuf, HID)
        sent(xb, X)
    sent(wmine.at[pl.ds(0, n - 1)], WA)
    for d in range(n):
        x_ = (x + d) % n
        ref = wbuf.at[x_, :, pl.ds(0, n - 1)] if d == 0 else wbuf.at[x_]
        pltpu.make_async_copy(ref, ref, send_w.at[x_]).wait()
    own_plane = (f_o == f) & (z_o == z)

    @pl.when(own_plane)
    def _():
        sent(wobuf.at[pl.ds(0, groups - 1)], WO)

    @pl.when(jnp.logical_not(own_plane))
    def _():
        sent(wobuf, WO)
    sent(most, KV)
    sent(zb.at[pl.ds(0, n - 1)], Z)
    sent(cache.at[:, :, pl.ds(0, (groups - 1) * run)], C)
    sent(ab.at[pl.ds(0, ranks - 1)], A)

    @pl.when(z == y)
    def _():
        sent(fin.at[pl.ds(0, ranks - 1)], FIN)

    @pl.when(z != y)
    def _():
        sent(fin, FIN)


def local(n, hidden, lengths, text_count, timestep, mod_table, w_qkv, w_out, qk_gain, stale_cache):
    nf = lax.axis_size("fsdp")
    patches, cd, width = hidden.shape
    rows_w, local_width = w_qkv.shape[1], w_qkv.shape[3]
    hl, groups, ranks = local_width // n, n * n, nf * n
    run = n * cd
    rows, out_w, own_rows, cap = patches * run, width // ranks, patches * cd, groups * run
    per = n * n * n // ranks
    mod = lax.dynamic_index_in_dim(mod_table[0], timestep[0], 0, keepdims=False).astype(F32)
    vmem, smem, anywhere = (pl.BlockSpec(memory_space=m) for m in (pltpu.VMEM, pltpu.SMEM, pl.ANY))
    out, cache = pl.pallas_call(
        functools.partial(relay, n, nf, patches, cd),
        out_shape=(
            jax.ShapeDtypeStruct((patches, cd, width), BF16),
            jax.ShapeDtypeStruct((2, patches, cap, local_width), BF16),
        ),
        in_specs=[vmem, smem, smem, vmem, vmem, vmem, vmem, anywhere],
        out_specs=(vmem, anywhere),
        scratch_shapes=[
            pltpu.VMEM((own_rows, width), BF16),
            pltpu.VMEM((n, own_rows, width), BF16),
            pltpu.VMEM((ranks, rows, out_w), BF16),
            pltpu.VMEM((rows, width), BF16),
            pltpu.VMEM((rows, width), BF16),
            pltpu.VMEM((n, rows_w, 3 * hl), BF16),
            pltpu.VMEM((n, n, n, rows_w, 3 * hl), BF16),
            pltpu.VMEM((nf * per, rows_w, local_width), BF16),
            pltpu.VMEM((groups, rows, 2 * hl), BF16),
            pltpu.VMEM((n, rows, 2 * hl), BF16),
            pltpu.VMEM((2, patches, run, local_width), BF16),
            pltpu.VMEM((ranks, rows, hl), BF16),
            pltpu.VMEM((rows, out_w), BF16),
            pltpu.VMEM((n, own_rows, out_w), BF16),
            pltpu.VMEM((ranks, own_rows, out_w), BF16),
            pltpu.VMEM((2, patches, cap, local_width), BF16),
            pltpu.VMEM((patches * cap, 2 * hl), BF16),
            pltpu.SemaphoreType.DMA((COPIES,)),
            pltpu.SemaphoreType.DMA((COPIES,)),
            pltpu.SemaphoreType.DMA((n,)),
            pltpu.SemaphoreType.DMA((n,)),
            pltpu.SemaphoreType.REGULAR,
        ],
        compiler_params=pltpu.CompilerParams(has_side_effects=True, vmem_limit_bytes=48 * 2**20),
    )(hidden, lengths, text_count, mod, w_qkv[0], w_out[0], qk_gain[0], stale_cache[0])
    return out[None], cache[None]


def solution(mesh):
    n = round(mesh.shape["tok"] ** (1 / 3))
    in_specs = (
        P(None, "tok", None),
        P(),
        P(),
        P(),
        P("section", None, None, None),
        P("section", "tok", None, "fsdp"),
        P("section", "tok", "fsdp"),
        P("section", None, None),
        P("section", None, None, None, "fsdp"),
    )
    out_specs = (P("section", None, "tok", None), P("section", None, None, None, "fsdp"))
    return jax.shard_map(
        functools.partial(local, n), mesh=mesh, in_specs=in_specs, out_specs=out_specs, check_vma=False
    )
```

time: 2400 us -> 215 us (0.09)
  the two profiles are of different devices: /device:TPU:40 before, /device:TPU:1 now
where the time goes in v1:
time: 215 us; the launch traced here: 214 us
  Pallas kernels  205 us (95%)
  local copies, waits for them, and re-layouts  6.74 us (3%)
    pallas_call x1, Pallas kernels, local(): pl.pallas_call(functools.partial(relay, n, nf, patches, cd), out_shape=(j...  205 us
    unnamed x13, local copies, waits for them, and re-layouts  6.65 us

profile of v1, /device:TPU:1, one launch (start us, length us, event | category | flops | bytes accessed | tf_op | source)
XLA Modules:
  0.0 213.9 jit_solution(11537354967131172313)
XLA Ops:
  0.6 0.0 copy-start
  2.1 0.1 copy-done
  2.2 0.1 constant_dynamic-slice_fusion
  2.3 1.1 copy.18
  3.4 0.0 copy-start.1
  3.5 0.9 copy-done.1
  4.3 0.0 copy-start.2
  4.3 0.9 copy-done.2
  5.2 0.0 copy-start.3
  5.2 0.7 copy-done.3
  5.9 0.0 copy-start.4
  5.9 0.7 copy-done.4
  6.6 205.1 %shard_map.104 = (bf16[4,4,3072]{2,1,0:T(4,128)(2,1)S(1)}, bf16[2,4,256,768]{3,2,1,0:T(8,128)(2,1)S(1)}) custom-call(bf16[4,4,3072]{2,1,0:T(4,128)(2,1)S(1)} %copy-done.1, s32[4]{0:T(128)S(1)} %copy-done.4, s32[1]{0:T(128)S(6)} %copy.21.text, f32[6,3072]{1,0:T(8,128)S(1)} %fusion.mod, bf16[48,3,768]{2,1,0:T(4,128)(2,1)S(1)} %bitcast.18, ...), custom_call_target="tpu_custom_call" | custom-call | tf_op jit(solution)/shard_map/pallas_call | solution.py:374
  211.6 0.6 copy.23
  212.3 1.7 copy.24
  (1 shorter events, 0.0 us)
Async XLA Ops:
  0.6 1.6 copy-start
  3.4 0.9 copy-start.1
  4.3 0.9 copy-start.2
  5.2 0.7 copy-start.3
  5.9 0.7 copy-start.4

commit v2 on v1

v2 whole, which is shorter than its diff:
```python
import functools

import jax
import jax.numpy as jnp
from jax import lax
from jax.experimental import pallas as pl
from jax.experimental.pallas import tpu as pltpu
from jax.sharding import PartitionSpec as P

HEAD_DIM = 64
F32 = jnp.float32
BF16 = jnp.bfloat16
HIDE = -1e30
HID, WA, KV, Z, A, F, X, FIN = range(8)
COPIES = 8
FETCHES = 7


def bits(number):
    assert number & (number - 1) == 0
    return number.bit_length() - 1


def matmul(a, b):
    return jnp.dot(a, b, preferred_element_type=F32)


def matmul_t(a, b):
    return lax.dot_general(a, b, (((1,), (1,)), ((), ())), preferred_element_type=F32)


def pick(index, values):
    out = jnp.zeros(index.shape, jnp.int32)
    for at, value in enumerate(values):
        out = jnp.where(index == at, value, out)
    return out


def relay(n, nf, patches, cd, hid_in, lens_in, text_in, time_in, mod_in, wq_in, wo_in, gain, stale, lo, cache,
          lens, text, time, hid, hmine, hbuf, xb, mod_all, mod, mb, wq, wmine, wbuf, wobuf, kv, zb, cb, ab, osum, osend,
          orecv, ob, fin, stl, old, fetches, sends, recvs, first, second, out_first, out_second, gate):
    width = hid.shape[-1]
    rows_w = wq.shape[1]
    local = wq.shape[2]
    hl = local // n
    hc = hl // HEAD_DIM
    groups = n * n
    ranks = nf * n
    out_w = width // ranks
    run = n * cd
    rows = patches * run
    cap = groups * run
    own_rows = patches * cd
    piece = width // groups

    s, f, t = lax.axis_index("section"), lax.axis_index("fsdp"), lax.axis_index("tok")
    x, z, y = t // (n * n), (t // n) % n, t % n
    g = x * n + y
    k = z * nf + f

    def to(x_, z_, y_, f_=None, s_=None):
        return {"section": s if s_ is None else s_, "fsdp": f if f_ is None else f_, "tok": (x_ * n + z_) * n + y_}

    def copy_to(src, dst, send, recv, target):
        return pltpu.make_async_remote_copy(
            src_ref=src, dst_ref=dst, send_sem=send, recv_sem=recv, device_id=target,
            device_id_type=pl.DeviceIdType.MESH)

    def remote(src, dst, which, target):
        return copy_to(src, dst, sends.at[which], recvs.at[which], target)

    def settle(ref, sem):
        pltpu.make_async_copy(ref, ref, sem).wait()

    def sent(ref, which):
        settle(ref, sends.at[which])

    def arrived(ref, which):
        settle(ref, recvs.at[which])

    def loop(low, high, body):
        def step(i, c):
            body(i)
            return c
        lax.fori_loop(low, high, step, 0)

    fetched = [pltpu.make_async_copy(a, b, fetches.at[i]) for i, (a, b) in enumerate(
        ((hid_in, hid), (wq_in, wq), (lens_in, lens), (text_in, text), (time_in, time), (mod_in, mod_all), (stale, stl)))]
    for fetch in fetched:
        fetch.start()

    barrier = pltpu.get_barrier_semaphore()

    def greet(target):
        pl.semaphore_signal(barrier, inc=1, device_id=target, device_id_type=pl.DeviceIdType.MESH)

    def greet_plane(d):
        g_ = (g + d) % groups
        greet(to(g_ // n, z, g_ % n))
    loop(1, groups, greet_plane)

    def greet_ring(d):
        k_ = (k + d) % ranks
        greet(to(x, k_ // nf, y, k_ % nf))
    loop(1, ranks, greet_ring)

    def greet_section(k_):
        greet(to(x, k_ // nf, y, k_ % nf, 1 - s))
    loop(0, ranks, greet_section)

    def greet_owner(j):
        j_, f_ = j // nf, j % nf

        @pl.when(jnp.logical_not((z == y) & (j_ == z) & (f_ == f)))
        def _():
            greet(to(x, j_, z, f_))
            greet(to(x, y, j_, f_))
    loop(0, ranks, greet_owner)

    r0 = lax.broadcasted_iota(jnp.int32, (rows, rows), 0)
    r1 = lax.broadcasted_iota(jnp.int32, (rows, rows), 1)

    def flipped(r):
        p_, y_, i_ = r >> bits(run), (r >> bits(cd)) & (n - 1), r & (cd - 1)
        return (y_ * patches + p_) * cd + i_

    fetched[1].wait()
    for z_ in range(n):
        for at, part in enumerate((2, 1, 0)):
            wmine[z_, :, at * hl:(at + 1) * hl] = wq[part, :, z_ * hl:(z_ + 1) * hl]
    fetched[0].wait()
    hmine[...] = hid[...].reshape(own_rows, width)

    plain = groups - 1 + ranks - 1 + ranks + 2 * ranks

    @pl.when(z == y)
    def _():
        pl.semaphore_wait(barrier, plain - 2)

    @pl.when(z != y)
    def _():
        pl.semaphore_wait(barrier, plain)

    def send(d):
        z_ = (z + d) % n
        remote(wmine.at[z_], wbuf.at[z, x, y], WA, to(x, z_, y)).start()
    loop(1, n, send)
    pltpu.make_async_copy(wmine.at[z], wbuf.at[z, x, y], recvs.at[WA]).start()
    put_wo = pltpu.make_async_copy(wo_in, wobuf.at[x, y], fetches.at[FETCHES])
    put_wo.start()

    @pl.when(s == 0)
    def _():
        def send(z_):
            same = (z_ == z) & (z == y)

            @pl.when(same)
            def _():
                pltpu.make_async_copy(hmine, hbuf.at[y], recvs.at[HID]).start()

            @pl.when(jnp.logical_not(same))
            def _():
                remote(hmine, hbuf.at[y], HID, to(x, z_, z)).start()
        loop(0, n, send)

    class Gather:
        def __init__(self, at, block, count):
            self.at, self.block, self.count = at, block, count

        def start(self):
            for half in range(2):
                mine = self.block(half, x, y)

                def send(d, half=half, mine=mine):
                    x_, y_ = (x + d) % n, (y + d) % n
                    along_x, along_y = to(x_, z, y), to(x, z, y_)
                    near, far = (along_x, along_y) if half == 0 else (along_y, along_x)
                    mark = x if half == 0 else y
                    copy_to(mine, mine, out_first.at[self.at, half], first.at[self.at, half, mark], near).start()
                    copy_to(mine, mine, out_second.at[self.at, half], second.at[self.at, half], far).start()
                loop(1, n, send)

        def forward(self):
            for d in range(1, n):
                for half in range(2):
                    mark = ((x if half == 0 else y) + d) % n
                    part = self.block(half, mark, y) if half == 0 else self.block(half, x, mark)
                    settle(part, first.at[self.at, half, mark])

                    def send(e, half=half, part=part):
                        far = to(x, z, (y + e) % n) if half == 0 else to((x + e) % n, z, y)
                        copy_to(part, part, out_second.at[self.at, half], second.at[self.at, half], far).start()
                    loop(1, n, send)

        def wait(self):
            for half in range(2):
                settle(self.count(half, n * (n - 1)), second.at[self.at, half])

        def close(self):
            for half in range(2):
                settle(self.count(half, n - 1), out_first.at[self.at, half])
                settle(self.count(half, n * (n - 1)), out_second.at[self.at, half])

    def count_of(ref, m):
        return ref(pl.ds(0, n), pl.ds(0, n - 1)) if m == n * (n - 1) else ref(0, pl.ds(0, n - 1))

    hz = n // 2
    w_gather = Gather(
        0, lambda half, x_, y_: wbuf.at[pl.ds(half * hz, hz), x_, y_],
        lambda half, m: count_of(lambda a, b: wbuf.at[pl.ds(half * hz, hz), a, b], m))
    wide = local // 2
    o_gather = Gather(
        1, lambda half, x_, y_: wobuf.at[x_, y_, :, pl.ds(half * wide, wide)],
        lambda half, m: count_of(lambda a, b: wobuf.at[a, b, :, pl.ds(half * wide, wide)], m))
    c_gather = Gather(
        2, lambda half, x_, y_: cache.at[half, :, pl.ds(pl.multiple_of((x_ * n + y_) * run, run), run)],
        lambda half, m: cache.at[half, :, pl.ds(0, m * run)])

    arrived(wmine, WA)

    @pl.when(s == 1)
    def _():
        pl.semaphore_wait(gate, 1)
    w_gather.start()
    put_wo.wait()
    w_gather.forward()
    o_gather.start()

    for at in (2, 3, 4, 5):
        fetched[at].wait()
    length = [lens[p] for p in range(patches)]
    begin = [sum(length[:p], jnp.int32(0)) for p in range(patches)]

    def about(at, count):
        row = at + lax.broadcasted_iota(jnp.int32, (count, 1), 0)
        row_patch = row >> bits(run)
        slot = g * run + (row & (run - 1))
        return slot < pick(row_patch, length), (pick(row_patch, begin) + slot) < text[0]

    live, is_text = about(0, rows)

    def regrouped(values):
        return jnp.concatenate(
            [values[:, (x_ * n + z_) * piece:(x_ * n + z_ + 1) * piece] for z_ in range(n) for x_ in range(n)], axis=1)

    steps = mod_all.shape[1]
    chosen = (lax.broadcasted_iota(jnp.int32, (8, steps), 1) == time[0]).astype(BF16)
    for c in range(mod_all.shape[0]):
        mod[c:c + 1, :] = regrouped(matmul(chosen, mod_all[c])[0:1])

    @pl.when(s == 0)
    def _():
        arrived(hbuf, HID)
        order = (flipped(r0) == r1).astype(BF16)
        states = regrouped(matmul(order, hbuf[...].reshape(rows, width)))
        for k_ in range(ranks):
            xb[k_] = states[:, k_ * out_w:(k_ + 1) * out_w].astype(BF16)

    @pl.when(s == 1)
    def _():
        arrived(xb, X)

    step = min(16, rows)
    for at in range(0, rows, step):
        here = slice(at, at + step)
        values = jnp.concatenate([xb[k_, here, :] for k_ in range(ranks)], axis=1).astype(F32)
        mean = jnp.mean(values, axis=1, keepdims=True)
        centred = values - mean
        spread = jnp.mean(centred * centred, axis=1, keepdims=True)
        normed = centred * lax.rsqrt(spread + 1e-05)
        text_here = about(at, step)[1]
        scale = jnp.where(text_here, mod[4:5, :], mod[1:2, :])
        shift = jnp.where(text_here, mod[3:4, :], mod[0:1, :])
        mb[here, :] = (normed * (1.0 + scale) + shift).astype(BF16)

    w_gather.wait()

    @pl.when(s == 0)
    def _():
        pl.semaphore_signal(gate, 1, device_id=to(x, z, y, f, 1), device_id_type=pl.DeviceIdType.MESH)
    total = matmul(mb[...], wbuf[...].reshape(width, 3 * hl))

    head = lax.broadcasted_iota(jnp.int32, (1, hl), 1) >> bits(HEAD_DIM)

    def head_norm(values, gains):
        mean = jnp.zeros_like(values)
        for h in range(hc):
            here = head == h
            mean = jnp.where(here, jnp.sum(jnp.where(here, values, 0.0), axis=1, keepdims=True) / HEAD_DIM, mean)
        centred = values - mean
        square = centred * centred
        spread = jnp.zeros_like(values)
        for h in range(hc):
            here = head == h
            spread = jnp.where(here, jnp.sum(jnp.where(here, square, 0.0), axis=1, keepdims=True) / HEAD_DIM, spread)
        return centred * lax.rsqrt(spread + 1e-06) * jnp.concatenate([gains] * hc, axis=1)

    value_new = jnp.where(live, total[:, :hl], 0.0)
    key_new = jnp.where(live, head_norm(total[:, hl:2 * hl], gain[1:2, :]), 0.0)
    kv[g] = jnp.concatenate([value_new, key_new], axis=1).astype(BF16)

    def send(d):
        g_ = (g + d) % groups
        remote(kv.at[g], kv.at[g], KV, to(g_ // n, z, g_ % n)).start()
    loop(1, groups, send)

    def send(d):
        z_ = (z + d) % n
        remote(kv.at[g], zb.at[z], Z, to(x, z_, y)).start()
    loop(1, n, send)
    pltpu.make_async_copy(kv.at[g], zb.at[z], recvs.at[Z]).start()

    query = head_norm(total[:, 2 * hl:], gain[0:1, :])
    query = jnp.concatenate([jnp.zeros((rows, hl), F32), query], axis=1)
    lane = lax.broadcasted_iota(jnp.int32, (1, 2 * hl), 1)
    queries = jnp.concatenate(
        [jnp.where(((lane - hl) >> bits(HEAD_DIM)) == h, query, 0.0) for h in range(hc)], axis=0).astype(BF16)
    query_row = lax.broadcasted_iota(jnp.int32, (hc * rows, 1), 0)
    query_patch = (query_row & (rows - 1)) >> bits(run)
    column = lax.broadcasted_iota(jnp.int32, (1, patches * cap), 1)

    fetched[6].wait()
    for z_ in range(n):
        @pl.when(z == z_)
        def _(z_=z_):
            mine = slice(z_ * hl, (z_ + 1) * hl)
            both = jnp.concatenate([stl[1, :, :, mine], stl[0, :, :, mine]], axis=2)
            old[...] = both.reshape(patches * cap, 2 * hl)
    old_patch = column >> bits(cap)
    old_seen = ((column & (cap - 1)) < pick(old_patch, length))
    score_old = matmul_t(queries, old[...]) * HEAD_DIM ** (-0.5)
    score_old = jnp.where(old_seen & (old_patch > query_patch), score_old, HIDE)
    top_old = jnp.max(score_old, axis=1, keepdims=True)

    o_gather.forward()

    most = kv.at[pl.ds(0, groups - 1)]
    arrived(most, KV)
    new = kv[...].reshape(patches * cap, 2 * hl)
    new_patch = (column >> bits(run)) & (patches - 1)
    new_slot = (column >> bits(rows)) * run + (column & (run - 1))
    new_seen = new_slot < pick(new_patch, length)
    score_new = matmul_t(queries, new) * HEAD_DIM ** (-0.5)
    score_new = jnp.where(new_seen & (new_patch <= query_patch), score_new, HIDE)
    top = jnp.maximum(top_old, jnp.max(score_new, axis=1, keepdims=True))
    expo_old, expo_new = jnp.exp(score_old - top), jnp.exp(score_new - top)
    norm = 1.0 / (jnp.sum(expo_old, axis=1, keepdims=True) + jnp.sum(expo_new, axis=1, keepdims=True))
    taken = matmul((expo_old * norm).astype(BF16), old[...]) + matmul((expo_new * norm).astype(BF16), new)
    attended = jnp.zeros((rows, hl), F32)
    for h in range(hc):
        attended = jnp.where(head == h, taken[h * rows:(h + 1) * rows, :hl], attended)
    ab[z] = attended.astype(BF16)

    def send(d):
        remote(ab.at[z], ab.at[z], A, to(x, (z + d) % n, y)).start()
    loop(1, n, send)

    arrived(zb, Z)
    both = jnp.concatenate([zb[z_][:, hl:] for z_ in range(n)], axis=1)
    cb[0] = both.reshape(patches, run, local)
    both = jnp.concatenate([zb[z_][:, :hl] for z_ in range(n)], axis=1)
    cb[1] = both.reshape(patches, run, local)
    put = pltpu.make_async_copy(cb, cache.at[:, :, pl.ds(pl.multiple_of(g * run, run), run)], fetches.at[FETCHES + 1])
    put.start()

    o_gather.wait()
    put.wait()
    c_gather.start()
    arrived(ab.at[pl.ds(0, n - 1)], A)
    left = jnp.concatenate([ab[z_] for z_ in range(n)], axis=1)
    projected = matmul_t(left, wobuf[...].reshape(nf * out_w, local))
    for f_ in range(nf):
        osum[f_] = projected[:, f_ * out_w:(f_ + 1) * out_w]
    osend[...] = osum[1 - f].astype(BF16)
    remote(osend, orecv, F, to(x, z, y, 1 - f)).start()
    c_gather.forward()
    arrived(orecv, F)
    projected = osum[f] + orecv[...].astype(F32)
    columns = pl.ds(pl.multiple_of(k * out_w, out_w), out_w)
    gated = jnp.where(is_text, mod[5:6, columns], mod[2:3, columns])
    result = jnp.where(live, xb[k].astype(F32) + gated * projected, 0.0).astype(BF16)

    @pl.when(s == 0)
    def _():
        hbuf_x = xb.at[k]
        hbuf_x[...] = result

        def send(k_):
            remote(xb.at[k], xb.at[k], X, to(x, k_ // nf, y, k_ % nf, 1)).start()
        loop(0, ranks, send)

    back = (r0 == flipped(r1)).astype(BF16)
    ob[...] = matmul(back, result).astype(BF16).reshape(n, own_rows, out_w)

    def send(j):
        y_, f_ = j // nf, j % nf
        same = (y_ == y) & (z == y) & (f_ == f)

        @pl.when(same)
        def _():
            pltpu.make_async_copy(ob.at[y_], fin.at[k], recvs.at[FIN]).start()

        @pl.when(jnp.logical_not(same))
        def _():
            remote(ob.at[y_], fin.at[k], FIN, to(x, y, y_, f_)).start()
    loop(0, ranks, send)

    arrived(fin, FIN)
    split = out_w // piece
    natural = [fin[z_ * nf + x_ // split][:, (x_ % split) * piece:(x_ % split + 1) * piece]
               for x_ in range(n) for z_ in range(n)]
    lo[...] = jnp.concatenate(natural, axis=1).reshape(patches, cd, width)
    c_gather.wait()

    @pl.when(s == 0)
    def _():
        @pl.when(z == y)
        def _():
            sent(hbuf.at[pl.ds(0, n - 1)], HID)

        @pl.when(z != y)
        def _():
            sent(hbuf, HID)
        sent(xb, X)
    sent(wmine.at[pl.ds(0, n - 1)], WA)
    for gather in (w_gather, o_gather, c_gather):
        gather.close()
    sent(most, KV)
    sent(zb.at[pl.ds(0, n - 1)], Z)
    sent(ab.at[pl.ds(0, n - 1)], A)
    sent(osend, F)

    @pl.when(z == y)
    def _():
        sent(fin.at[pl.ds(0, ranks - 1)], FIN)

    @pl.when(z != y)
    def _():
        sent(fin, FIN)


def local(n, hidden, lengths, text_count, timestep, mod_table, w_qkv, w_out, qk_gain, stale_cache):
    nf = lax.axis_size("fsdp")
    patches, cd, width = hidden.shape
    rows_w, local_width = w_qkv.shape[1], w_qkv.shape[3]
    hl, groups, ranks = local_width // n, n * n, nf * n
    run = n * cd
    rows, out_w, own_rows, cap = patches * run, width // ranks, patches * cd, groups * run
    steps, kinds = mod_table.shape[1:3]
    vmem, anywhere = pl.BlockSpec(memory_space=pltpu.VMEM), pl.BlockSpec(memory_space=pl.ANY)
    out, cache = pl.pallas_call(
        functools.partial(relay, n, nf, patches, cd),
        out_shape=(
            jax.ShapeDtypeStruct((patches, cd, width), BF16),
            jax.ShapeDtypeStruct((2, patches, cap, local_width), BF16),
        ),
        in_specs=[anywhere] * 7 + [vmem, anywhere],
        out_specs=(vmem, anywhere),
        scratch_shapes=[
            pltpu.SMEM((patches,), jnp.int32),
            pltpu.SMEM((1,), jnp.int32),
            pltpu.SMEM((1,), jnp.int32),
            pltpu.VMEM((patches, cd, width), BF16),
            pltpu.VMEM((own_rows, width), BF16),
            pltpu.VMEM((n, own_rows, width), BF16),
            pltpu.VMEM((ranks, rows, out_w), BF16),
            pltpu.VMEM((kinds, steps, width), BF16),
            pltpu.VMEM((kinds, width), F32),
            pltpu.VMEM((rows, width), BF16),
            pltpu.VMEM((3, rows_w, local_width), BF16),
            pltpu.VMEM((n, rows_w, 3 * hl), BF16),
            pltpu.VMEM((n, n, n, rows_w, 3 * hl), BF16),
            pltpu.VMEM((n, n, rows_w, local_width), BF16),
            pltpu.VMEM((groups, rows, 2 * hl), BF16),
            pltpu.VMEM((n, rows, 2 * hl), BF16),
            pltpu.VMEM((2, patches, run, local_width), BF16),
            pltpu.VMEM((n, rows, hl), BF16),
            pltpu.VMEM((nf, rows, out_w), F32),
            pltpu.VMEM((rows, out_w), BF16),
            pltpu.VMEM((rows, out_w), BF16),
            pltpu.VMEM((n, own_rows, out_w), BF16),
            pltpu.VMEM((ranks, own_rows, out_w), BF16),
            pltpu.VMEM((2, patches, cap, local_width), BF16),
            pltpu.VMEM((patches * cap, 2 * hl), BF16),
            pltpu.SemaphoreType.DMA((FETCHES + 2,)),
            pltpu.SemaphoreType.DMA((COPIES,)),
            pltpu.SemaphoreType.DMA((COPIES,)),
            pltpu.SemaphoreType.DMA((3, 2, n)),
            pltpu.SemaphoreType.DMA((3, 2)),
            pltpu.SemaphoreType.DMA((3, 2)),
            pltpu.SemaphoreType.DMA((3, 2)),
            pltpu.SemaphoreType.REGULAR,
        ],
        compiler_params=pltpu.CompilerParams(
            collective_id=0, has_side_effects=True, vmem_limit_bytes=48 * 2**20),
    )(hidden, lengths, text_count, timestep, jnp.swapaxes(mod_table[0], 0, 1), jnp.swapaxes(w_qkv[0], 0, 1), w_out[0],
      qk_gain[0], stale_cache[0])
    return out[None], cache[None]


def solution(mesh):
    n = round(mesh.shape["tok"] ** (1 / 3))
    in_specs = (
        P(None, "tok", None),
        P(),
        P(),
        P(),
        P("section", None, None, None),
        P("section", "tok", None, "fsdp"),
        P("section", "tok", "fsdp"),
        P("section", None, None),
        P("section", None, None, None, "fsdp"),
    )
    out_specs = (P("section", None, "tok", None), P("section", None, None, None, "fsdp"))
    return jax.shard_map(
        functools.partial(local, n), mesh=mesh, in_specs=in_specs, out_specs=out_specs, check_vma=False
    )
```

time: 215 us -> 113 us (0.53)
  Pallas kernels: 205 us -> 103 us
    pallas_call x1, Pallas kernels: 205 us -> 103 us  [local(): pl.pallas_call(functools.partial(relay, n, nf, patches, cd), out_shape=(j...]
    unnamed x13 -> x14, local copies, waits for them, and re-layouts: 6.65 us -> 7.92 us
where the time goes in v2:
time: 113 us
  Pallas kernels  103 us (91%)
  local copies, waits for them, and re-layouts  7.92 us (7%)
  between operations  1.95 us (2%)
    pallas_call x1, Pallas kernels, local(): pl.pallas_call(functools.partial(relay, n, nf, patches, cd), out_shape=(j...  103 us
    unnamed x14, local copies, waits for them, and re-layouts  7.92 us

profile of v2, /device:TPU:1, one launch (start us, length us, event | category | flops | bytes accessed | tf_op | source)
XLA Modules:
  0.0 112.6 jit_solution(16563881826266353520)
XLA Ops:
  1.9 0.0 copy-start
  1.9 1.6 %copy-done = bf16[1,50,6,3072]{3,1,2,0:T(8,128)(2,1)S(1)} copy-done((bf16[1,50,6,3072]{3,1,2,0:T(8,128)(2,1)S(1)}, bf16[1,50,6,3072]{3,1,2,0:T(8,128)(2,1)}, u32[]{:S(2)}) %copy-start) | copy-done | bytes 1843224
  3.5 0.0 copy-start.1
  3.5 0.9 copy-done.1
  4.4 0.0 copy-start.2
  4.4 0.9 copy-done.2
  5.3 0.0 copy-start.3
  5.3 0.9 copy-done.3
  6.2 0.0 copy-start.4
  6.2 0.7 copy-done.4
  6.9 0.0 copy-start.5
  6.9 0.7 copy-done.5
  7.6 102.7 %shard_map.104 = (bf16[4,4,3072]{2,1,0:T(4,128)(2,1)S(1)}, bf16[2,4,256,768]{3,2,1,0:T(8,128)(2,1)S(1)}) custom-call(bf16[4,4,3072]{2,1,0:T(4,128)(2,1)S(1)} %copy-done.2, s32[4]{0:T(128)S(1)} %copy-done.5, s32[1]{0:T(128)S(6)} %copy.13.text_in, s32[1]{0:T(128)S(6)} %copy.14.time_in, bf16[6,50,3072]{2,1,0:T(8,128)(2,1)S(1)} %bitcast.12, ...), custom_call_target="tpu_custom_call" | custom-call | tf_op jit(solution)/shard_map/pallas_call | solution.py:451
  110.3 0.6 copy.15
  110.9 1.7 %copy.16 = bf16[1,2,4,256,768]{4,3,2,1,0:T(8,128)(2,1)} copy(bf16[1,2,4,256,768]{4,3,2,1,0:T(8,128)(2,1)S(1)} %bitcast.11) | data formatting | bytes 6291456
Async XLA Ops:
  1.9 1.6 %copy-start = (bf16[1,50,6,3072]{3,1,2,0:T(8,128)(2,1)S(1)}, bf16[1,50,6,3072]{3,1,2,0:T(8,128)(2,1)}, u32[]{:S(2)}) copy-start(bf16[1,50,6,3072]{3,1,2,0:T(8,128)(2,1)} %param.13) | copy-start | bytes 5529604
  3.5 0.9 copy-start.1
  4.4 0.9 copy-start.2
  5.3 0.9 copy-start.3
  6.2 0.7 copy-start.4
  6.9 0.7 copy-start.5

commit v3 on v2

--- a/solution.py
+++ b/solution.py
@@ -11,8 +11,8 @@
 F32 = jnp.float32
 BF16 = jnp.bfloat16
 HIDE = -1e30
-HID, WA, KV, Z, A, F, X, FIN = range(8)
-COPIES = 8
+HID, WA, KV, Z, A, F, X, FIN, MS, RS = range(10)
+COPIES = 10
 FETCHES = 7
 
 
@@ -37,8 +37,8 @@
 
 
 def relay(n, nf, patches, cd, hid_in, lens_in, text_in, time_in, mod_in, wq_in, wo_in, gain, stale, lo, cache,
-          lens, text, time, hid, hmine, hbuf, xb, mod_all, mod, mb, wq, wmine, wbuf, wobuf, kv, zb, cb, ab, osum, osend,
-          orecv, ob, fin, stl, old, fetches, sends, recvs, first, second, out_first, out_second, gate):
+          lens, text, time, hid, mine_m, all_m, mine_h, xres, xb, mod_all, mod_in_order, mod, mb, wq, wmine, wbuf, wobuf,
+          part_all, part_send, part_recv, total_ref, kv, zb, cb, ab, osum, osend, orecv, ob, fin, stl, old, fetches, sends, recvs, first, second, out_first, out_second, gate):
     width = hid.shape[-1]
     rows_w = wq.shape[1]
     local = wq.shape[2]
@@ -108,14 +108,11 @@
         greet(to(x, k_ // nf, y, k_ % nf, 1 - s))
     loop(0, ranks, greet_section)
 
-    def greet_owner(j):
-        j_, f_ = j // nf, j % nf
-
-        @pl.when(jnp.logical_not((z == y) & (j_ == z) & (f_ == f)))
-        def _():
-            greet(to(x, j_, z, f_))
-            greet(to(x, y, j_, f_))
-    loop(0, ranks, greet_owner)
+    def greet_planes(j):
+        d, z_ = 1 + j // (n - 1), (z + 1 + j % (n - 1)) % n
+        greet(to((x + d) % n, z_, y))
+        greet(to(x, z_, (y + d) % n))
+    loop(0, (n - 1) ** 2, greet_planes)
 
     r0 = lax.broadcasted_iota(jnp.int32, (rows, rows), 0)
     r1 = lax.broadcasted_iota(jnp.int32, (rows, rows), 1)
@@ -128,18 +125,54 @@
     for z_ in range(n):
         for at, part in enumerate((2, 1, 0)):
             wmine[z_, :, at * hl:(at + 1) * hl] = wq[part, :, z_ * hl:(z_ + 1) * hl]
-    fetched[0].wait()
-    hmine[...] = hid[...].reshape(own_rows, width)
-
-    plain = groups - 1 + ranks - 1 + ranks + 2 * ranks
-
-    @pl.when(z == y)
-    def _():
-        pl.semaphore_wait(barrier, plain - 2)
-
-    @pl.when(z != y)
-    def _():
-        pl.semaphore_wait(barrier, plain)
+
+    for at in (0, 2, 3, 4, 5):
+        fetched[at].wait()
+    length = [lens[p] for p in range(patches)]
+    begin = [sum(length[:p], jnp.int32(0)) for p in range(patches)]
+
+    def about(first_z, count):
+        row = lax.broadcasted_iota(jnp.int32, (count, 1), 0)
+        row_patch = (row >> bits(cd)) & (patches - 1)
+        slot = ((x * n + first_z + (row >> bits(own_rows))) * n + y) * cd + (row & (cd - 1))
+        return slot < pick(row_patch, length), (pick(row_patch, begin) + slot) < text[0]
+
+    live, is_text = about(0, rows)
+
+    def feature(values, x_, z_):
+        return values[:, (x_ * n + z_) * piece:(x_ * n + z_ + 1) * piece]
+
+    steps = mod_all.shape[1]
+    chosen = (lax.broadcasted_iota(jnp.int32, (8, steps), 1) == time[0]).astype(BF16)
+    for c in range(mod_all.shape[0]):
+        values = matmul(chosen, mod_all[c])[0:1]
+        mod_in_order[c:c + 1, :] = values
+        mod[c:c + 1, :] = jnp.concatenate([feature(values, x_, z_) for z_ in range(n) for x_ in range(n)], axis=1)
+
+    def modulated(values, text_here, table):
+        mean = jnp.mean(values, axis=1, keepdims=True)
+        centred = values - mean
+        spread = jnp.mean(centred * centred, axis=1, keepdims=True)
+        normed = centred * lax.rsqrt(spread + 1e-05)
+        scale = jnp.where(text_here, table[4:5, :], table[1:2, :])
+        shift = jnp.where(text_here, table[3:4, :], table[0:1, :])
+        return (normed * (1.0 + scale) + shift).astype(BF16)
+
+    chunk = n * piece
+    split = out_w // piece
+
+    @pl.when(s == 0)
+    def _():
+        states = hid[...].reshape(own_rows, width)
+        normed = modulated(states.astype(F32), about(z, own_rows)[1], mod_in_order)
+        for x_ in range(n):
+            mine_m[x_] = normed[:, x_ * chunk:(x_ + 1) * chunk]
+        for f_ in range(nf):
+            for z_ in range(n):
+                mine_h[f_, z_] = jnp.concatenate(
+                    [feature(states, f_ * split + e, z_) for e in range(split)], axis=1)
+
+    pl.semaphore_wait(barrier, groups - 1 + ranks - 1 + ranks + 2 * (n - 1) ** 2)
 
     def send(d):
         z_ = (z + d) % n
@@ -151,17 +184,24 @@
 
     @pl.when(s == 0)
     def _():
-        def send(z_):
-            same = (z_ == z) & (z == y)
+        def send(j):
+            x_, z_ = j // n, j % n
+            same = (x_ == x) & (z_ == z)
 
             @pl.when(same)
             def _():
-                pltpu.make_async_copy(hmine, hbuf.at[y], recvs.at[HID]).start()
+                pltpu.make_async_copy(mine_m.at[x], all_m.at[x * n + z], recvs.at[MS]).start()
 
             @pl.when(jnp.logical_not(same))
             def _():
-                remote(hmine, hbuf.at[y], HID, to(x, z_, z)).start()
-        loop(0, n, send)
+                remote(mine_m.at[x_], all_m.at[x * n + z], MS, to(x_, z_, y)).start()
+        loop(0, groups, send)
+
+        def send(d):
+            z_ = (z + d) % n
+            remote(mine_h.at[f, z_], xres.at[z], HID, to(x, z_, y)).start()
+        loop(1, n, send)
+        pltpu.make_async_copy(mine_h.at[f, z], xres.at[z], recvs.at[HID]).start()
 
     class Gather:
         def __init__(self, at, block, count):
@@ -217,68 +257,50 @@
         lambda half, m: cache.at[half, :, pl.ds(0, m * run)])
 
     arrived(wmine, WA)
+    most_w = wbuf.at[:, 0, pl.ds(0, n - 1)]
+
+    @pl.when(s == 0)
+    def _():
+        def send(d):
+            part = wbuf.at[:, x, y]
+            copy_to(part, part, out_second.at[0, 0], second.at[0, 0], to(x, z, (y + d) % n)).start()
+        loop(1, n, send)
+        put_wo.wait()
+        o_gather.start()
+        arrived(all_m, MS)
+        settle(most_w, second.at[0, 0])
+        pl.semaphore_signal(gate, 1, device_id=to(x, z, y, f, 1), device_id_type=pl.DeviceIdType.MESH)
+        weight = wbuf[:, x].reshape(chunk, 3 * hl)
+        for x_ in range(n):
+            part = matmul(all_m[x_ * n:(x_ + 1) * n].reshape(rows, chunk), weight)
+            part_all[x_] = part
+            part_send[x_] = part.astype(BF16)
+
+        def send(d):
+            x_ = (x + d) % n
+            remote(part_send.at[x_], part_recv.at[x], RS, to(x_, z, y)).start()
+        loop(1, n, send)
+        arrived(part_recv.at[pl.ds(0, n - 1)], RS)
+        total = part_all[x]
+        for d in range(1, n):
+            total = total + part_recv[(x + d) % n].astype(F32)
+        total_ref[...] = total
 
     @pl.when(s == 1)
     def _():
         pl.semaphore_wait(gate, 1)
-    w_gather.start()
-    put_wo.wait()
-    w_gather.forward()
-    o_gather.start()
-
-    for at in (2, 3, 4, 5):
-        fetched[at].wait()
-    length = [lens[p] for p in range(patches)]
-    begin = [sum(length[:p], jnp.int32(0)) for p in range(patches)]
-
-    def about(at, count):
-        row = at + lax.broadcasted_iota(jnp.int32, (count, 1), 0)
-        row_patch = row >> bits(run)
-        slot = g * run + (row & (run - 1))
-        return slot < pick(row_patch, length), (pick(row_patch, begin) + slot) < text[0]
-
-    live, is_text = about(0, rows)
-
-    def regrouped(values):
-        return jnp.concatenate(
-            [values[:, (x_ * n + z_) * piece:(x_ * n + z_ + 1) * piece] for z_ in range(n) for x_ in range(n)], axis=1)
-
-    steps = mod_all.shape[1]
-    chosen = (lax.broadcasted_iota(jnp.int32, (8, steps), 1) == time[0]).astype(BF16)
-    for c in range(mod_all.shape[0]):
-        mod[c:c + 1, :] = regrouped(matmul(chosen, mod_all[c])[0:1])
-
-    @pl.when(s == 0)
-    def _():
-        arrived(hbuf, HID)
-        order = (flipped(r0) == r1).astype(BF16)
-        states = regrouped(matmul(order, hbuf[...].reshape(rows, width)))
-        for k_ in range(ranks):
-            xb[k_] = states[:, k_ * out_w:(k_ + 1) * out_w].astype(BF16)
-
-    @pl.when(s == 1)
-    def _():
+        w_gather.start()
+        put_wo.wait()
+        w_gather.forward()
+        o_gather.start()
         arrived(xb, X)
-
-    step = min(16, rows)
-    for at in range(0, rows, step):
-        here = slice(at, at + step)
-        values = jnp.concatenate([xb[k_, here, :] for k_ in range(ranks)], axis=1).astype(F32)
-        mean = jnp.mean(values, axis=1, keepdims=True)
-        centred = values - mean
-        spread = jnp.mean(centred * centred, axis=1, keepdims=True)
-        normed = centred * lax.rsqrt(spread + 1e-05)
-        text_here = about(at, step)[1]
-        scale = jnp.where(text_here, mod[4:5, :], mod[1:2, :])
-        shift = jnp.where(text_here, mod[3:4, :], mod[0:1, :])
-        mb[here, :] = (normed * (1.0 + scale) + shift).astype(BF16)
-
-    w_gather.wait()
-
-    @pl.when(s == 0)
-    def _():
-        pl.semaphore_signal(gate, 1, device_id=to(x, z, y, f, 1), device_id_type=pl.DeviceIdType.MESH)
-    total = matmul(mb[...], wbuf[...].reshape(width, 3 * hl))
+        for at in range(n):
+            here = slice(at * own_rows, (at + 1) * own_rows)
+            values = jnp.concatenate([xb[k_, here, :] for k_ in range(ranks)], axis=1).astype(F32)
+            mb[here, :] = modulated(values, about(at, own_rows)[1], mod)
+        w_gather.wait()
+        total_ref[...] = matmul(mb[...], wbuf[...].reshape(width, 3 * hl))
+    total = total_ref[...]
 
     head = lax.broadcasted_iota(jnp.int32, (1, hl), 1) >> bits(HEAD_DIM)
 
@@ -305,10 +327,18 @@
     loop(1, groups, send)
 
     def send(d):
-        z_ = (z + d) % n
-        remote(kv.at[g], zb.at[z], Z, to(x, z_, y)).start()
-    loop(1, n, send)
-    pltpu.make_async_copy(kv.at[g], zb.at[z], recvs.at[Z]).start()
+        own_z, z_ = d // n, d % n
+        part = kv.at[g, pl.ds(pl.multiple_of(own_z * own_rows, own_rows), own_rows)]
+        same = (own_z == y) & (z_ == z)
+
+        @pl.when(same)
+        def _():
+            pltpu.make_async_copy(part, zb.at[z * n + y], recvs.at[Z]).start()
+
+        @pl.when(jnp.logical_not(same))
+        def _():
+            remote(part, zb.at[z * n + y], Z, to(x, z_, own_z)).start()
+    loop(0, groups, send)
 
     query = head_norm(total[:, 2 * hl:], gain[0:1, :])
     query = jnp.concatenate([jnp.zeros((rows, hl), F32), query], axis=1)
@@ -316,7 +346,7 @@
     queries = jnp.concatenate(
         [jnp.where(((lane - hl) >> bits(HEAD_DIM)) == h, query, 0.0) for h in range(hc)], axis=0).astype(BF16)
     query_row = lax.broadcasted_iota(jnp.int32, (hc * rows, 1), 0)
-    query_patch = (query_row & (rows - 1)) >> bits(run)
+    query_patch = (query_row >> bits(cd)) & (patches - 1)
     column = lax.broadcasted_iota(jnp.int32, (1, patches * cap), 1)
 
     fetched[6].wait()
@@ -337,8 +367,10 @@
     most = kv.at[pl.ds(0, groups - 1)]
     arrived(most, KV)
     new = kv[...].reshape(patches * cap, 2 * hl)
-    new_patch = (column >> bits(run)) & (patches - 1)
-    new_slot = (column >> bits(rows)) * run + (column & (run - 1))
+    new_patch = (column >> bits(cd)) & (patches - 1)
+    new_group, new_z = column >> bits(rows), (column >> bits(own_rows)) & (n - 1)
+    new_tok = ((new_group >> bits(n)) * n + new_z) * n + (new_group & (n - 1))
+    new_slot = new_tok * cd + (column & (cd - 1))
     new_seen = new_slot < pick(new_patch, length)
     score_new = matmul_t(queries, new) * HEAD_DIM ** (-0.5)
     score_new = jnp.where(new_seen & (new_patch <= query_patch), score_new, HIDE)
@@ -356,10 +388,10 @@
     loop(1, n, send)
 
     arrived(zb, Z)
-    both = jnp.concatenate([zb[z_][:, hl:] for z_ in range(n)], axis=1)
-    cb[0] = both.reshape(patches, run, local)
-    both = jnp.concatenate([zb[z_][:, :hl] for z_ in range(n)], axis=1)
-    cb[1] = both.reshape(patches, run, local)
+    order = (flipped(r0) == r1).astype(BF16)
+    for at, lanes in enumerate((slice(hl, 2 * hl), slice(0, hl))):
+        both = jnp.concatenate([zb[z_ * n:(z_ + 1) * n].reshape(rows, 2 * hl)[:, lanes] for z_ in range(n)], axis=1)
+        cb[at] = matmul(order, both).astype(BF16).reshape(patches, run, local)
     put = pltpu.make_async_copy(cb, cache.at[:, :, pl.ds(pl.multiple_of(g * run, run), run)], fetches.at[FETCHES + 1])
     put.start()
 
@@ -378,65 +410,56 @@
     projected = osum[f] + orecv[...].astype(F32)
     columns = pl.ds(pl.multiple_of(k * out_w, out_w), out_w)
     gated = jnp.where(is_text, mod[5:6, columns], mod[2:3, columns])
+
+    @pl.when(s == 0)
+    def _():
+        arrived(xres, HID)
+        xb[k] = xres[...].reshape(rows, out_w)
     result = jnp.where(live, xb[k].astype(F32) + gated * projected, 0.0).astype(BF16)
+    ob[...] = result
 
     @pl.when(s == 0)
     def _():
-        hbuf_x = xb.at[k]
-        hbuf_x[...] = result
-
         def send(k_):
-            remote(xb.at[k], xb.at[k], X, to(x, k_ // nf, y, k_ % nf, 1)).start()
+            remote(ob, xb.at[k], X, to(x, k_ // nf, y, k_ % nf, 1)).start()
         loop(0, ranks, send)
 
-    back = (r0 == flipped(r1)).astype(BF16)
-    ob[...] = matmul(back, result).astype(BF16).reshape(n, own_rows, out_w)
-
-    def send(j):
-        y_, f_ = j // nf, j % nf
-        same = (y_ == y) & (z == y) & (f_ == f)
-
-        @pl.when(same)
-        def _():
-            pltpu.make_async_copy(ob.at[y_], fin.at[k], recvs.at[FIN]).start()
-
-        @pl.when(jnp.logical_not(same))
-        def _():
-            remote(ob.at[y_], fin.at[k], FIN, to(x, y, y_, f_)).start()
-    loop(0, ranks, send)
+    def own(z_):
+        return ob.at[pl.ds(pl.multiple_of(z_ * own_rows, own_rows), own_rows)]
+
+    def send(d):
+        k_ = (k + d) % ranks
+        remote(own(k_ // nf), fin.at[k], FIN, to(x, k_ // nf, y, k_ % nf)).start()
+    loop(1, ranks, send)
+    pltpu.make_async_copy(own(z), fin.at[k], recvs.at[FIN]).start()
 
     arrived(fin, FIN)
-    split = out_w // piece
     natural = [fin[z_ * nf + x_ // split][:, (x_ % split) * piece:(x_ % split + 1) * piece]
                for x_ in range(n) for z_ in range(n)]
     lo[...] = jnp.concatenate(natural, axis=1).reshape(patches, cd, width)
     c_gather.wait()
 
+    sent(wmine.at[pl.ds(0, n - 1)], WA)
+
     @pl.when(s == 0)
     def _():
-        @pl.when(z == y)
-        def _():
-            sent(hbuf.at[pl.ds(0, n - 1)], HID)
-
-        @pl.when(z != y)
-        def _():
-            sent(hbuf, HID)
+        sent(all_m.at[0:groups - 1], MS)
+        sent(xres.at[pl.ds(0, n - 1)], HID)
+        settle(most_w, out_second.at[0, 0])
+        sent(part_send.at[pl.ds(0, n - 1)], RS)
         sent(xb, X)
-    sent(wmine.at[pl.ds(0, n - 1)], WA)
-    for gather in (w_gather, o_gather, c_gather):
-        gather.close()
+
+    @pl.when(s == 1)
+    def _():
+        w_gather.close()
+    o_gather.close()
+    c_gather.close()
     sent(most, KV)
-    sent(zb.at[pl.ds(0, n - 1)], Z)
+    sent(zb.at[0:groups - 1], Z)
     sent(ab.at[pl.ds(0, n - 1)], A)
     sent(osend, F)
 
-    @pl.when(z == y)
-    def _():
-        sent(fin.at[pl.ds(0, ranks - 1)], FIN)
-
-    @pl.when(z != y)
-    def _():
-        sent(fin, FIN)
+    sent(fin.at[pl.ds(0, ranks - 1)], FIN)
 
 
 def local(n, hidden, lengths, text_count, timestep, mod_table, w_qkv, w_out, qk_gain, stale_cache):
@@ -461,24 +484,31 @@
             pltpu.SMEM((1,), jnp.int32),
             pltpu.SMEM((1,), jnp.int32),
             pltpu.VMEM((patches, cd, width), BF16),
-            pltpu.VMEM((own_rows, width), BF16),
-            pltpu.VMEM((n, own_rows, width), BF16),
+            pltpu.VMEM((n, own_rows, width // n), BF16),
+            pltpu.VMEM((groups, own_rows, width // n), BF16),
+            pltpu.VMEM((nf, n, own_rows, out_w), BF16),
+            pltpu.VMEM((n, own_rows, out_w), BF16),
             pltpu.VMEM((ranks, rows, out_w), BF16),
             pltpu.VMEM((kinds, steps, width), BF16),
+            pltpu.VMEM((kinds, width), F32),
             pltpu.VMEM((kinds, width), F32),
             pltpu.VMEM((rows, width), BF16),
             pltpu.VMEM((3, rows_w, local_width), BF16),
             pltpu.VMEM((n, rows_w, 3 * hl), BF16),
             pltpu.VMEM((n, n, n, rows_w, 3 * hl), BF16),
             pltpu.VMEM((n, n, rows_w, local_width), BF16),
+            pltpu.VMEM((n, rows, 3 * hl), F32),
+            pltpu.VMEM((n, rows, 3 * hl), BF16),
+            pltpu.VMEM((n, rows, 3 * hl), BF16),
+            pltpu.VMEM((rows, 3 * hl), F32),
             pltpu.VMEM((groups, rows, 2 * hl), BF16),
-            pltpu.VMEM((n, rows, 2 * hl), BF16),
+            pltpu.VMEM((groups, own_rows, 2 * hl), BF16),
             pltpu.VMEM((2, patches, run, local_width), BF16),
             pltpu.VMEM((n, rows, hl), BF16),
             pltpu.VMEM((nf, rows, out_w), F32),
             pltpu.VMEM((rows, out_w), BF16),
             pltpu.VMEM((rows, out_w), BF16),
-            pltpu.VMEM((n, own_rows, out_w), BF16),
+            pltpu.VMEM((rows, out_w), BF16),
             pltpu.VMEM((ranks, own_rows, out_w), BF16),
             pltpu.VMEM((2, patches, cap, local_width), BF16),
             pltpu.VMEM((patches * cap, 2 * hl), BF16),
@@ -492,7 +522,7 @@
             pltpu.SemaphoreType.REGULAR,
         ],
         compiler_params=pltpu.CompilerParams(
-            collective_id=0, has_side_effects=True, vmem_limit_bytes=48 * 2**20),
+            collective_id=0, has_side_effects=True, vmem_limit_bytes=62 * 2**20),
     )(hidden, lengths, text_count, timestep, jnp.swapaxes(mod_table[0], 0, 1), jnp.swapaxes(w_qkv[0], 0, 1), w_out[0],
       qk_gain[0], stale_cache[0])
     return out[None], cache[None]

time: 113 us -> 105 us (0.929)
  Pallas kernels: 103 us -> 97.9 us
  local copies, waits for them, and re-layouts: 7.92 us -> 5.32 us
    pallas_call x1, Pallas kernels: 103 us -> 97.9 us  [local(): pl.pallas_call(functools.partial(relay, n, nf, patches, cd), out_shape=(j...]
    unnamed x14 -> x2, local copies, waits for them, and re-layouts: 7.92 us -> 5.32 us
where the time goes in v3:
time: 105 us
  Pallas kernels  97.9 us (93%)
  local copies, waits for them, and re-layouts  5.32 us (5%)
  between operations  1.93 us (2%)
    pallas_call x1, Pallas kernels, local(): pl.pallas_call(functools.partial(relay, n, nf, patches, cd), out_shape=(j...  97.9 us
    unnamed x2, local copies, waits for them, and re-layouts  5.32 us

profile of v3, /device:TPU:1, one launch (start us, length us, event | category | flops | bytes accessed | tf_op | source)
XLA Modules:
  0.0 105.2 jit_solution(3526275737899580336)
XLA Ops:
  1.9 97.9 %shard_map.104 = (bf16[4,4,3072]{2,1,0:T(4,128)(2,1)}, bf16[2,4,256,768]{3,2,1,0:T(8,128)(2,1)}) custom-call(bf16[4,4,3072]{2,1,0:T(4,128)(2,1)} %hid_in.1, s32[4]{0:T(128)} %lens_in.1, s32[1]{0:T(128)S(6)} %copy.13.text_in, s32[1]{0:T(128)S(6)} %copy.14.time_in, bf16[6,50,3072]{2,1,0:T(8,128)(2,1)} %bitcast.13, bf16[3,48,768]{2,1,0:T(8,128)(2,1)} %bitcast.14, ...), custom_call_target="tpu_custom_call" | custom-call | tf_op jit(solution)/shard_map/pallas_call | solution.py:474
  99.8 1.6 %copy.15 = bf16[1,4,4,3072]{3,2,1,0:T(4,128)(2,1)} copy(bf16[1,4,4,3072]{3,2,1,0:T(4,128)(2,1)} %bitcast.15) | data formatting | bytes 196608
  101.4 3.8 %copy.16 = bf16[1,2,4,256,768]{4,3,2,1,0:T(8,128)(2,1)} copy(bf16[1,2,4,256,768]{4,3,2,1,0:T(8,128)(2,1)} %bitcast.11) | data formatting | bytes 6291456

commit v4 on v3

--- a/solution.py
+++ b/solution.py
@@ -11,8 +11,8 @@
 F32 = jnp.float32
 BF16 = jnp.bfloat16
 HIDE = -1e30
-HID, WA, KV, Z, A, F, X, FIN, MS, RS = range(10)
-COPIES = 10
+HID, WA, Z, A, F, X, FIN, MS, RS = range(9)
+COPIES = 9
 FETCHES = 7
 
 
@@ -38,7 +38,7 @@
 
 def relay(n, nf, patches, cd, hid_in, lens_in, text_in, time_in, mod_in, wq_in, wo_in, gain, stale, lo, cache,
           lens, text, time, hid, mine_m, all_m, mine_h, xres, xb, mod_all, mod_in_order, mod, mb, wq, wmine, wbuf, wobuf,
-          part_all, part_send, part_recv, total_ref, kv, zb, cb, ab, osum, osend, orecv, ob, fin, stl, old, fetches, sends, recvs, first, second, out_first, out_second, gate):
+          part_all, part_send, part_recv, total_ref, kv, zb, ab, osum, osend, orecv, ob, fin, cv, stl, old, fetches, sends, recvs, first, second, out_first, out_second, put_sems, gate):
     width = hid.shape[-1]
     rows_w = wq.shape[1]
     local = wq.shape[2]
@@ -252,9 +252,13 @@
     o_gather = Gather(
         1, lambda half, x_, y_: wobuf.at[x_, y_, :, pl.ds(half * wide, wide)],
         lambda half, m: count_of(lambda a, b: wobuf.at[a, b, :, pl.ds(half * wide, wide)], m))
+    hr = rows // 2
+    kv_gather = Gather(
+        3, lambda half, x_, y_: kv.at[x_ * n + y_, pl.ds(half * hr, hr)],
+        lambda half, m: kv.at[pl.ds(0, m), pl.ds(half * hr, hr)])
     c_gather = Gather(
-        2, lambda half, x_, y_: cache.at[half, :, pl.ds(pl.multiple_of((x_ * n + y_) * run, run), run)],
-        lambda half, m: cache.at[half, :, pl.ds(0, m * run)])
+        2, lambda half, x_, y_: cv.at[half, :, pl.ds(pl.multiple_of((x_ * n + y_) * run, run), run)],
+        lambda half, m: cv.at[half, :, pl.ds(0, m * run)])
 
     arrived(wmine, WA)
     most_w = wbuf.at[:, 0, pl.ds(0, n - 1)]
@@ -321,10 +325,7 @@
     key_new = jnp.where(live, head_norm(total[:, hl:2 * hl], gain[1:2, :]), 0.0)
     kv[g] = jnp.concatenate([value_new, key_new], axis=1).astype(BF16)
 
-    def send(d):
-        g_ = (g + d) % groups
-        remote(kv.at[g], kv.at[g], KV, to(g_ // n, z, g_ % n)).start()
-    loop(1, groups, send)
+    kv_gather.start()
 
     def send(d):
         own_z, z_ = d // n, d % n
@@ -358,14 +359,14 @@
             old[...] = both.reshape(patches * cap, 2 * hl)
     old_patch = column >> bits(cap)
     old_seen = ((column & (cap - 1)) < pick(old_patch, length))
+    kv_gather.forward()
     score_old = matmul_t(queries, old[...]) * HEAD_DIM ** (-0.5)
     score_old = jnp.where(old_seen & (old_patch > query_patch), score_old, HIDE)
     top_old = jnp.max(score_old, axis=1, keepdims=True)
 
     o_gather.forward()
 
-    most = kv.at[pl.ds(0, groups - 1)]
-    arrived(most, KV)
+    kv_gather.wait()
     new = kv[...].reshape(patches * cap, 2 * hl)
     new_patch = (column >> bits(cd)) & (patches - 1)
     new_group, new_z = column >> bits(rows), (column >> bits(own_rows)) & (n - 1)
@@ -391,12 +392,9 @@
     order = (flipped(r0) == r1).astype(BF16)
     for at, lanes in enumerate((slice(hl, 2 * hl), slice(0, hl))):
         both = jnp.concatenate([zb[z_ * n:(z_ + 1) * n].reshape(rows, 2 * hl)[:, lanes] for z_ in range(n)], axis=1)
-        cb[at] = matmul(order, both).astype(BF16).reshape(patches, run, local)
-    put = pltpu.make_async_copy(cb, cache.at[:, :, pl.ds(pl.multiple_of(g * run, run), run)], fetches.at[FETCHES + 1])
-    put.start()
+        cv[at, :, pl.ds(pl.multiple_of(g * run, run), run), :] = matmul(order, both).astype(BF16).reshape(patches, run, local)
 
     o_gather.wait()
-    put.wait()
     c_gather.start()
     arrived(ab.at[pl.ds(0, n - 1)], A)
     left = jnp.concatenate([ab[z_] for z_ in range(n)], axis=1)
@@ -438,6 +436,9 @@
                for x_ in range(n) for z_ in range(n)]
     lo[...] = jnp.concatenate(natural, axis=1).reshape(patches, cd, width)
     c_gather.wait()
+    puts = [pltpu.make_async_copy(cv.at[c, p], cache.at[c, p], put_sems.at[c, p]) for c in range(2) for p in range(patches)]
+    for put in puts:
+        put.start()
 
     sent(wmine.at[pl.ds(0, n - 1)], WA)
 
@@ -454,12 +455,30 @@
         w_gather.close()
     o_gather.close()
     c_gather.close()
-    sent(most, KV)
+    kv_gather.close()
     sent(zb.at[0:groups - 1], Z)
     sent(ab.at[pl.ds(0, n - 1)], A)
     sent(osend, F)
 
     sent(fin.at[pl.ds(0, ranks - 1)], FIN)
+    for put in puts:
+        put.wait()
+
+
+def hand_back(out, cache, lo, new_cache, out_v, cache_v, sems):
+    parts = [(out, out_v, lo)]
+    for c in range(cache.shape[0]):
+        for p in range(cache.shape[1]):
+            parts.append((cache.at[c, p], cache_v.at[c, p], new_cache.at[c, p]))
+    fetches = [pltpu.make_async_copy(a, b, sems.at[0, i]) for i, (a, b, _) in enumerate(parts)]
+    puts = [pltpu.make_async_copy(b, c, sems.at[1, i]) for i, (_, b, c) in enumerate(parts)]
+    for fetch in fetches:
+        fetch.start()
+    for fetch, put in zip(fetches, puts):
+        fetch.wait()
+        put.start()
+    for put in puts:
+        put.wait()
 
 
 def local(n, hidden, lengths, text_count, timestep, mod_table, w_qkv, w_out, qk_gain, stale_cache):
@@ -503,7 +522,6 @@
             pltpu.VMEM((rows, 3 * hl), F32),
             pltpu.VMEM((groups, rows, 2 * hl), BF16),
             pltpu.VMEM((groups, own_rows, 2 * hl), BF16),
-            pltpu.VMEM((2, patches, run, local_width), BF16),
             pltpu.VMEM((n, rows, hl), BF16),
             pltpu.VMEM((nf, rows, out_w), F32),
             pltpu.VMEM((rows, out_w), BF16),
@@ -511,20 +529,34 @@
             pltpu.VMEM((rows, out_w), BF16),
             pltpu.VMEM((ranks, own_rows, out_w), BF16),
             pltpu.VMEM((2, patches, cap, local_width), BF16),
+            pltpu.VMEM((2, patches, cap, local_width), BF16),
             pltpu.VMEM((patches * cap, 2 * hl), BF16),
-            pltpu.SemaphoreType.DMA((FETCHES + 2,)),
+            pltpu.SemaphoreType.DMA((FETCHES + 1,)),
             pltpu.SemaphoreType.DMA((COPIES,)),
             pltpu.SemaphoreType.DMA((COPIES,)),
-            pltpu.SemaphoreType.DMA((3, 2, n)),
-            pltpu.SemaphoreType.DMA((3, 2)),
-            pltpu.SemaphoreType.DMA((3, 2)),
-            pltpu.SemaphoreType.DMA((3, 2)),
+            pltpu.SemaphoreType.DMA((4, 2, n)),
+            pltpu.SemaphoreType.DMA((4, 2)),
+            pltpu.SemaphoreType.DMA((4, 2)),
+            pltpu.SemaphoreType.DMA((4, 2)),
+            pltpu.SemaphoreType.DMA((2, patches)),
             pltpu.SemaphoreType.REGULAR,
         ],
         compiler_params=pltpu.CompilerParams(
             collective_id=0, has_side_effects=True, vmem_limit_bytes=62 * 2**20),
     )(hidden, lengths, text_count, timestep, jnp.swapaxes(mod_table[0], 0, 1), jnp.swapaxes(w_qkv[0], 0, 1), w_out[0],
       qk_gain[0], stale_cache[0])
+    out, cache = pl.pallas_call(
+        hand_back,
+        out_shape=(jax.ShapeDtypeStruct(out.shape, BF16), jax.ShapeDtypeStruct(cache.shape, BF16)),
+        in_specs=[anywhere] * 2,
+        out_specs=(anywhere, anywhere),
+        scratch_shapes=[
+            pltpu.VMEM(out.shape, BF16),
+            pltpu.VMEM(cache.shape, BF16),
+            pltpu.SemaphoreType.DMA((2, 1 + 2 * patches)),
+        ],
+        compiler_params=pltpu.CompilerParams(vmem_limit_bytes=62 * 2**20),
+    )(out, cache)
     return out[None], cache[None]
 
 

time: 105 us -> 103 us (0.981)
  local copies, waits for them, and re-layouts: 5.32 us -> 0 us
  Pallas kernels: 97.9 us -> 100 us
    unnamed x2 -> x0, local copies, waits for them, and re-layouts: 5.32 us -> none
    pallas_call x0 -> x1, Pallas kernels: none -> 2.86 us  [local(): pl.pallas_call(hand_back, out_shape=(jax.ShapeDtypeStruct(out.shape, BF16...]
where the time goes in v4:
time: 103 us; the launch traced here: 102 us
  Pallas kernels  100 us (97%)
  between operations  1.93 us (2%)
    pallas_call x1, Pallas kernels, local(): pl.pallas_call(functools.partial(relay, n, nf, patches, cd), out_shape=(j...  97.6 us
    pallas_call x1, Pallas kernels, local(): pl.pallas_call(hand_back, out_shape=(jax.ShapeDtypeStruct(out.shape, BF16...  2.86 us

profile of v4, /device:TPU:1, one launch (start us, length us, event | category | flops | bytes accessed | tf_op | source)
XLA Modules:
  0.0 102.4 jit_solution(12776710342890011945)
XLA Ops:
  1.9 97.6 %shard_map.104 = (bf16[4,4,3072]{2,1,0:T(4,128)(2,1)}, bf16[2,4,256,768]{3,2,1,0:T(8,128)(2,1)}) custom-call(bf16[4,4,3072]{2,1,0:T(4,128)(2,1)} %hid_in.1, s32[4]{0:T(128)} %lens_in.1, s32[1]{0:T(128)S(6)} %copy.11.text_in, s32[1]{0:T(128)S(6)} %copy.12.time_in, bf16[6,50,3072]{2,1,0:T(8,128)(2,1)} %bitcast.12, bf16[3,48,768]{2,1,0:T(8,128)(2,1)} %bitcast.13, ...), custom_call_target="tpu_custom_call" | custom-call | tf_op jit(solution)/shard_map/pallas_call | solution.py:493
  99.6 2.9 %shard_map.105 = (bf16[4,4,3072]{2,1,0:T(4,128)(2,1)}, bf16[2,4,256,768]{3,2,1,0:T(8,128)(2,1)}) custom-call(bf16[4,4,3072]{2,1,0:T(4,128)(2,1)} %get-tuple-element.6.out, bf16[2,4,256,768]{3,2,1,0:T(8,128)(2,1)} %get-tuple-element.7.cache), custom_call_target="tpu_custom_call" | custom-call | tf_op jit(solution)/shard_map/pallas_call | solution.py:548

commit v5 on v4

--- a/solution.py
+++ b/solution.py
@@ -275,10 +275,9 @@
         settle(most_w, second.at[0, 0])
         pl.semaphore_signal(gate, 1, device_id=to(x, z, y, f, 1), device_id_type=pl.DeviceIdType.MESH)
         weight = wbuf[:, x].reshape(chunk, 3 * hl)
-        for x_ in range(n):
-            part = matmul(all_m[x_ * n:(x_ + 1) * n].reshape(rows, chunk), weight)
-            part_all[x_] = part
-            part_send[x_] = part.astype(BF16)
+        parts = matmul(all_m[...].reshape(n * rows, chunk), weight).reshape(n, rows, 3 * hl)
+        part_send[...] = parts.astype(BF16)
+        part_all[...] = parts
 
         def send(d):
             x_ = (x + d) % n
@@ -365,6 +364,18 @@
     top_old = jnp.max(score_old, axis=1, keepdims=True)
 
     o_gather.forward()
+
+    def assemble():
+        arrived(zb, Z)
+        order = (flipped(r0) == r1).astype(BF16)
+        for at, lanes in enumerate((slice(hl, 2 * hl), slice(0, hl))):
+            both = jnp.concatenate([zb[z_ * n:(z_ + 1) * n].reshape(rows, 2 * hl)[:, lanes] for z_ in range(n)], axis=1)
+            cv[at, :, pl.ds(pl.multiple_of(g * run, run), run), :] = matmul(order, both).astype(BF16).reshape(patches, run, local)
+        c_gather.start()
+
+    @pl.when(s == 1)
+    def _():
+        assemble()
 
     kv_gather.wait()
     new = kv[...].reshape(patches * cap, 2 * hl)
@@ -388,14 +399,15 @@
         remote(ab.at[z], ab.at[z], A, to(x, (z + d) % n, y)).start()
     loop(1, n, send)
 
-    arrived(zb, Z)
-    order = (flipped(r0) == r1).astype(BF16)
-    for at, lanes in enumerate((slice(hl, 2 * hl), slice(0, hl))):
-        both = jnp.concatenate([zb[z_ * n:(z_ + 1) * n].reshape(rows, 2 * hl)[:, lanes] for z_ in range(n)], axis=1)
-        cv[at, :, pl.ds(pl.multiple_of(g * run, run), run), :] = matmul(order, both).astype(BF16).reshape(patches, run, local)
+    @pl.when(s == 1)
+    def _():
+        c_gather.forward()
+
+    @pl.when(s == 0)
+    def _():
+        assemble()
 
     o_gather.wait()
-    c_gather.start()
     arrived(ab.at[pl.ds(0, n - 1)], A)
     left = jnp.concatenate([ab[z_] for z_ in range(n)], axis=1)
     projected = matmul_t(left, wobuf[...].reshape(nf * out_w, local))
@@ -403,7 +415,7 @@
         osum[f_] = projected[:, f_ * out_w:(f_ + 1) * out_w]
     osend[...] = osum[1 - f].astype(BF16)
     remote(osend, orecv, F, to(x, z, y, 1 - f)).start()
-    c_gather.forward()
+
     arrived(orecv, F)
     projected = osum[f] + orecv[...].astype(F32)
     columns = pl.ds(pl.multiple_of(k * out_w, out_w), out_w)
@@ -431,6 +443,9 @@
     loop(1, ranks, send)
     pltpu.make_async_copy(own(z), fin.at[k], recvs.at[FIN]).start()
 
+    @pl.when(s == 0)
+    def _():
+        c_gather.forward()
     arrived(fin, FIN)
     natural = [fin[z_ * nf + x_ // split][:, (x_ % split) * piece:(x_ % split + 1) * piece]
                for x_ in range(n) for z_ in range(n)]

time: 103 us -> 99.4 us (0.965)
  Pallas kernels: 100 us -> 97.4 us
    pallas_call x1, Pallas kernels: 97.6 us -> 94.5 us  [local(): pl.pallas_call(functools.partial(relay, n, nf, patches, cd), out_shape=(j...]
where the time goes in v5:
time: 99.4 us; the launch traced here: 99.3 us
  Pallas kernels  97.4 us (98%)
  between operations  1.93 us (2%)
    pallas_call x1, Pallas kernels, local(): pl.pallas_call(functools.partial(relay, n, nf, patches, cd), out_shape=(j...  94.5 us
    pallas_call x1, Pallas kernels, local(): pl.pallas_call(hand_back, out_shape=(jax.ShapeDtypeStruct(out.shape, BF16...  2.86 us

profile of v5, /device:TPU:1, one launch (start us, length us, event | category | flops | bytes accessed | tf_op | source)
XLA Modules:
  0.0 99.3 jit_solution(4108768500992129220)
XLA Ops:
  1.9 94.5 %shard_map.104 = (bf16[4,4,3072]{2,1,0:T(4,128)(2,1)}, bf16[2,4,256,768]{3,2,1,0:T(8,128)(2,1)}) custom-call(bf16[4,4,3072]{2,1,0:T(4,128)(2,1)} %hid_in.1, s32[4]{0:T(128)} %lens_in.1, s32[1]{0:T(128)S(6)} %copy.11.text_in, s32[1]{0:T(128)S(6)} %copy.12.time_in, bf16[6,50,3072]{2,1,0:T(8,128)(2,1)} %bitcast.12, bf16[3,48,768]{2,1,0:T(8,128)(2,1)} %bitcast.13, ...), custom_call_target="tpu_custom_call" | custom-call | tf_op jit(solution)/shard_map/pallas_call | solution.py:508
  96.4 2.9 %shard_map.105 = (bf16[4,4,3072]{2,1,0:T(4,128)(2,1)}, bf16[2,4,256,768]{3,2,1,0:T(8,128)(2,1)}) custom-call(bf16[4,4,3072]{2,1,0:T(4,128)(2,1)} %get-tuple-element.6.out, bf16[2,4,256,768]{3,2,1,0:T(8,128)(2,1)} %get-tuple-element.7.cache), custom_call_target="tpu_custom_call" | custom-call | tf_op jit(solution)/shard_map/pallas_call | solution.py:563

commit v6 on v5

--- a/solution.py
+++ b/solution.py
@@ -296,6 +296,7 @@
         put_wo.wait()
         w_gather.forward()
         o_gather.start()
+        o_gather.forward()
         arrived(xb, X)
         for at in range(n):
             here = slice(at * own_rows, (at + 1) * own_rows)
@@ -363,7 +364,10 @@
     score_old = jnp.where(old_seen & (old_patch > query_patch), score_old, HIDE)
     top_old = jnp.max(score_old, axis=1, keepdims=True)
 
-    o_gather.forward()
+
+    @pl.when(s == 0)
+    def _():
+        o_gather.forward()
 
     def assemble():
         arrived(zb, Z)

time: 99.4 us -> 98.9 us (level)
  no operation moved by 1% of the time
where the time goes in v6:
time: 98.9 us; the launch traced here: 98.8 us
  Pallas kernels  96.8 us (98%)
  between operations  1.93 us (2%)
    pallas_call x1, Pallas kernels, local(): pl.pallas_call(functools.partial(relay, n, nf, patches, cd), out_shape=(j...  94 us
    pallas_call x1, Pallas kernels, local(): pl.pallas_call(hand_back, out_shape=(jax.ShapeDtypeStruct(out.shape, BF16...  2.86 us

profile of v6, /device:TPU:1, one launch (start us, length us, event | category | flops | bytes accessed | tf_op | source)
XLA Modules:
  0.0 98.8 jit_solution(18194829472209661664)
XLA Ops:
  1.9 94.0 %shard_map.104 = (bf16[4,4,3072]{2,1,0:T(4,128)(2,1)}, bf16[2,4,256,768]{3,2,1,0:T(8,128)(2,1)}) custom-call(bf16[4,4,3072]{2,1,0:T(4,128)(2,1)} %hid_in.1, s32[4]{0:T(128)} %lens_in.1, s32[1]{0:T(128)S(6)} %copy.11.text_in, s32[1]{0:T(128)S(6)} %copy.12.time_in, bf16[6,50,3072]{2,1,0:T(8,128)(2,1)} %bitcast.12, bf16[3,48,768]{2,1,0:T(8,128)(2,1)} %bitcast.13, ...), custom_call_target="tpu_custom_call" | custom-call | tf_op jit(solution)/shard_map/pallas_call | solution.py:512
  95.9 2.9 %shard_map.105 = (bf16[4,4,3072]{2,1,0:T(4,128)(2,1)}, bf16[2,4,256,768]{3,2,1,0:T(8,128)(2,1)}) custom-call(bf16[4,4,3072]{2,1,0:T(4,128)(2,1)} %get-tuple-element.6.out, bf16[2,4,256,768]{3,2,1,0:T(8,128)(2,1)} %get-tuple-element.7.cache), custom_call_target="tpu_custom_call" | custom-call | tf_op jit(solution)/shard_map/pallas_call | solution.py:567
